TPU v7x, 512 devices: a whole 4x4x16 slice. The times are simulated.
512 devices in a mesh: gx: 4 (over y), gy: 16 (over z_hi, x, core), gz: 8 (over z_lo).
Axes of the slice: x: 4, y: 4, z: 16 (z_hi: 2, z_lo: 8; z = z_hi * 8 + z_lo), core: 2. Of those that a mesh axis runs over, the one named last changes fastest.
Arguments:
- moving_image: bfloat16 [64, 128, 4096], P('gz', 'gx', 'gy'), may hold values from -6 to 6
- moving_grad: bfloat16 [3, 64, 128, 4096], P(None, 'gz', 'gx', 'gy'), may hold values from -6 to 6
- fixed_grad: bfloat16 [3, 64, 128, 4096], P(None, 'gz', 'gx', 'gy'), may hold values from -6 to 6
- voxel_weight: bfloat16 [64, 128, 4096], P('gz', 'gx', 'gy'), may hold values from 0.01 to 40, as said below
- coefficients: float32 [8, 4, 16, 3, 128], P('gz', 'gx', 'gy'), may hold values from -1 to 1
- weight_table: bfloat16 [8, 256, 128], replicated, may hold values from 0 to 1, as said below
- ctrl_slot: int32 [8, 4, 16, 256, 8], P('gz', 'gx', 'gy'), may hold values from 0 to 26, as said below
- weight_slot: int32 [8, 4, 16, 256, 8], P('gz', 'gx', 'gy'), may hold values from 0 to 7
Outputs:
- new_coefficients: float32 [8, 4, 16, 3, 128], P('gz', 'gx', 'gy')
- warped_image: float32 [64, 128, 4096], P('gz', 'gx', 'gy')
- energies: float32 [2], replicated
Inputs may be any that keep to these rules, and one draw needn't show every extreme that they name: `ctrl_slot`: an entry s equals 13 + 9 * dz + 3 * dx + dy, where dz, dx and dy, each -1, 0 or 1, are the offsets of the owning tile along the plane groups, the tile columns and the tile rows, so that s = 13 is the tile itself; for slot k of a block, dz is 0 if bit 2 of k is 0 and else the side of the tile's nearer z face (-1 for the lower half of its planes, +1 for the upper); dx likewise by bit 1 of k and the nearer x face; dy is 0 if bit 0 of k is 0 and else -1 or +1; slot 0 of every block is 13. `voxel_weight`: positive weights. `weight_table`: each entry is a product of cubic B-spline basis values along z, x and y between a voxel of the row and a control point.
All inputs are finite; a program needn't handle non-finite values.
Results may differ from a plain program's by a relative error of at most 0.0003.
Values may be sent and summed in bfloat16 or wider, within the bound.
A program may use at most 64 MiB of HBM per device.

v0:
```python
import jax
import jax.numpy as jnp
from jax import lax
from jax.sharding import PartitionSpec as P

STEPS = 2


EDGE_SQUARED = 0.05
STEP_LENGTH = 0.05
FULL_PRECISION = lax.Precision.HIGHEST


def padded_2(cells, sides, width):
    for axis, dim in sides:
        count = lax.axis_size(axis)
        ends = count - 1
        head = lax.slice_in_dim(cells, 0, width, axis=dim)
        tail = lax.slice_in_dim(cells, cells.shape[dim] - width, cells.shape[dim], axis=dim)
        cells = jnp.concatenate(
            [
                lax.ppermute(tail, axis, [(i, (i + 1) % count) for i in range(ends)]),
                cells,
                lax.ppermute(head, axis, [((i + 1) % count, i) for i in range(ends)]),
            ],
            axis=dim,
        )
    return cells


def central_grad(padded):
    along_z = (padded[2:, 1:-1, 1:-1] - padded[:-2, 1:-1, 1:-1]) * 0.5
    along_x = (padded[1:-1, 2:, 1:-1] - padded[1:-1, :-2, 1:-1]) * 0.5
    along_y = (padded[1:-1, 1:-1, 2:] - padded[1:-1, 1:-1, :-2]) * 0.5
    return (along_z, along_x, along_y)


def adjoint_divergence(flux_padded):
    return (
        flux_padded[0, :-2, 1:-1, 1:-1]
        - flux_padded[0, 2:, 1:-1, 1:-1]
        + (flux_padded[1, 1:-1, :-2, 1:-1] - flux_padded[1, 1:-1, 2:, 1:-1])
        + (flux_padded[2, 1:-1, 1:-1, :-2] - flux_padded[2, 1:-1, 1:-1, 2:])
    ) * 0.5


def gradient_flux(grads, fixed_three, weights):
    inner = grads[0] * fixed_three[0] + grads[1] * fixed_three[1] + grads[2] * fixed_three[2]
    fixed_sq = fixed_three[0] ** 2 + fixed_three[1] ** 2 + fixed_three[2] ** 2 + EDGE_SQUARED
    moving_sq = grads[0] ** 2 + grads[1] ** 2 + grads[2] ** 2 + EDGE_SQUARED
    denominator = fixed_sq * moving_sq
    terms = weights * (1.0 - inner * inner / denominator)
    first_part = -2.0 * weights * inner / denominator
    second_part = 2.0 * weights * inner * inner / (denominator * moving_sq)
    flux = jnp.stack(
        [
            first_part * fixed_three[component] + second_part * grads[component]
            for component in range(3)
        ]
    )
    return (terms, flux)


def on_device(
    moving_image,
    moving_grad,
    fixed_grad,
    voxel_weight,
    coefficients,
    weight_table,
    ctrl_slot,
    weight_slot,
):
    plane_count, row_count, column_count = moving_image.shape
    table_count, block_length, ctrl_count = weight_table.shape
    slot_count = ctrl_slot.shape[-1]
    block_count = plane_count * row_count
    device_count = lax.axis_size("gx") * lax.axis_size("gy") * lax.axis_size("gz")
    voxels_all = plane_count * row_count * column_count * device_count
    table_wide = weight_table.astype(jnp.float32)
    combined = ctrl_slot[0, 0, 0] * table_count + weight_slot[0, 0, 0]
    targets = jnp.arange(27 * table_count, dtype=jnp.int32)[None, :]
    picker = jnp.zeros((block_count, 27 * table_count), jnp.float32)
    for slot_index in range(slot_count):
        picker = picker + (combined[:, slot_index][:, None] == targets).astype(jnp.float32)
    current = coefficients
    energy_list = []
    warped = None
    for step_index in range(STEPS):
        neighbourhood = padded_2(current, (("gx", 1), ("gy", 2), ("gz", 0)), 1)
        neighbourhood = neighbourhood.reshape(27, 3, ctrl_count)
        block_products = jnp.einsum(
            "sjc,nvc->snjv", neighbourhood, table_wide, precision=FULL_PRECISION
        )
        block_products = block_products.reshape(27 * table_count, 3 * block_length)
        field = jnp.zeros((block_count, 3 * block_length), jnp.float32)
        for slot_index in range(slot_count):
            field = field + jnp.take(block_products, combined[:, slot_index], axis=0)
        field = field.reshape(plane_count, row_count, 3, column_count)
        warped = (
            moving_image.astype(jnp.float32)
            + field[:, :, 0, :] * moving_grad[0]
            + field[:, :, 1, :] * moving_grad[1]
            + field[:, :, 2, :] * moving_grad[2]
        )
        padded = padded_2(warped, (("gx", 1), ("gy", 2), ("gz", 0)), 1)
        grads = central_grad(padded)
        terms, flux = gradient_flux(
            grads, fixed_grad.astype(jnp.float32), voxel_weight.astype(jnp.float32)
        )
        flux_padded = padded_2(flux, (("gx", 2), ("gy", 3), ("gz", 1)), 1)
        pulled = adjoint_divergence(flux_padded)
        local_energy = jnp.sum(terms)
        energy_total = lax.psum(local_energy, ("gx", "gy", "gz"))
        weighted = jnp.stack([pulled * moving_grad[component] for component in range(3)], axis=2)
        weighted = weighted.reshape(block_count, 3 * block_length)
        grouped = jnp.einsum("bm,bx->mx", picker, weighted, precision=FULL_PRECISION)
        grouped = grouped.reshape(27, table_count, 3, block_length)
        partials = jnp.einsum("snjv,nvc->sjc", grouped, table_wide, precision=FULL_PRECISION)
        partials = partials.reshape(3, 3, 3, 3, ctrl_count)
        summed = padded_2(partials, (("gx", 1), ("gy", 2), ("gz", 0)), 1)
        gradient = jnp.sum(summed[0::2, 0::2, 0::2], axis=(0, 1, 2))
        local_square = jnp.sum(gradient * gradient)
        square_total = lax.psum(local_square, ("gx", "gy", "gz"))
        energy_list.append(energy_total / float(voxels_all))
        step_size = STEP_LENGTH / jnp.sqrt(
            square_total / float(device_count * 3 * ctrl_count) + 1e-06
        )
        current = current - step_size * gradient[None, None, None]
    return (current, warped, jnp.stack(energy_list))


def solution(mesh):
    in_specs = (
        P("gz", "gx", "gy"),
        P(None, "gz", "gx", "gy"),
        P(None, "gz", "gx", "gy"),
        P("gz", "gx", "gy"),
        P("gz", "gx", "gy", None, None),
        P(),
        P("gz", "gx", "gy", None, None),
        P("gz", "gx", "gy", None, None),
    )
    out_specs = (P("gz", "gx", "gy", None, None), P("gz", "gx", "gy"), P())
    return jax.shard_map(
        on_device, mesh=mesh, in_specs=in_specs, out_specs=out_specs, check_vma=False
    )
```

profile of v0, /device:TPU:1, one launch (start us, length us, event | category | flops | bytes accessed | tf_op | source)
XLA Modules:
  0.0 620.8 jit_solution(774695315779905429)
XLA Ops:
  2.1 4.7 collective-permute-start
  8.6 9.1 %collective-permute-start.3 = (f32[1,3,1,3,128]{4,2,3,1,0:T(1,128)S(1)}, f32[1,3,1,3,128]{4,2,3,1,0:T(1,128)S(1)}, u32[]{:S(2)}, u32[]{:S(2)}) collective-permute-start(f32[1,3,1,3,128]{4,2,3,1,0:T(1,128)S(1)} %constant_dynamic-update-slice_fusion), channel_id=1, source_target_pairs={{8,0},{16,8},{24,16},{32,24},{40,32},{48,40},{56,48},{64,56},{72,6... | collective-permute-start | bytes 13832 | tf_op jit(solution)/shard_map/ppermute | solution.py:24
  17.6 1.9 collective-permute-start.2
  22.0 4.0 collective-permute-start.4
  29.3 2.0 gather_fusion.6
  31.3 2.0 gather_fusion.5
  33.2 2.0 gather_fusion.4
  35.2 2.0 gather_fusion.3
  37.2 2.0 gather_fusion.2
  39.2 2.0 gather_fusion.1
  41.1 2.0 gather_fusion
  43.2 2.9 select_add_fusion.7
  47.7 4.0 collective-permute-start.6
  53.1 3.1 collective-permute-done.7
  56.3 6.5 %collective-permute-start.8 = (f32[8,34,1]{2,1,0:T(8,128)S(1)}, f32[8,34,1]{2,1,0:T(8,128)S(1)}, u32[]{:S(2)}, u32[]{:S(2)}) collective-permute-start(f32[8,34,1]{2,1,0:T(8,128)S(1)} %get-tuple-element.59), channel_id=1, source_target_pairs={{0,8},{8,16},{16,24},{24,32},{32,40},{40,48},{48,56},{56,64},{64,7... | collective-permute-start | bytes 3272 | tf_op jit(solution)/shard_map/ppermute | solution.py:22
  62.8 1.9 collective-permute-start.9
  65.0 4.4 collective-permute-done.9
  70.9 4.6 collective-permute-start.11
  81.4 3.3 collective-permute-done.13
  85.0 4.0 collective-permute-start.14
  89.0 1.9 collective-permute-start.15
  91.0 3.8 collective-permute-done.14
  94.8 4.4 collective-permute-done.15
  99.4 4.3 collective-permute-start.16
  107.0 3.3 collective-permute-done.17
  116.4 3.2 collective-permute-done.19
  119.6 4.1 collective-permute-start.20
  123.8 1.9 collective-permute-start.21
  125.7 3.6 collective-permute-done.21
  129.4 3.5 collective-permute-start.22
  134.2 5.5 collective-permute-done.23
  141.4 169.5 %psum.28 = f32[]{:T(128)} all-reduce(f32[]{:T(128)} %multiply_reduce_fusion.1), channel_id=1, replica_groups=mesh['gx'=4,'gy'=16,'gz'=8] {'gx','gy','gz'}, use_global_device_ids=true, to_apply=%region_2.4 | all-reduce | flops 1 | bytes 8 | tf_op jit(solution)/shard_map/psum | solution.py:124
  313.0 4.0 collective-permute-start.24
  317.7 3.7 collective-permute-start.27
  321.4 3.0 collective-permute-start.26
  326.5 4.0 collective-permute-start.28
  332.7 2.1 gather_fusion.15
  334.8 2.1 gather_fusion.14
  336.9 2.1 gather_fusion.13
  339.0 2.1 gather_fusion.12
  341.1 2.1 gather_fusion.11
  343.2 2.1 gather_fusion.10
  345.3 2.1 gather_fusion.9
  347.5 2.1 gather_fusion.8
  349.6 3.1 select_add_fusion
  355.8 4.5 collective-permute-start.30
  361.3 6.2 collective-permute-start.32
  369.7 4.4 collective-permute-done.33
  375.5 4.6 collective-permute-start.35
  382.9 3.9 collective-permute-start.36
  388.1 3.5 collective-permute-done.37
  391.9 4.0 collective-permute-start.38
  395.9 1.9 collective-permute-start.39
  397.9 3.8 collective-permute-done.38
  401.7 4.4 collective-permute-done.39
  406.3 4.4 collective-permute-start.40
  413.2 3.8 collective-permute-done.41
  420.6 3.6 collective-permute-start.42
  425.6 3.2 collective-permute-done.43
  428.8 4.6 collective-permute-start.44
  435.3 3.2 collective-permute-done.45
  438.5 3.3 collective-permute-start.46
  443.1 5.6 collective-permute-done.47
  450.5 167.3 %all-reduce = (f32[]{:T(128)}, f32[]{:T(128)}, f32[]{:T(128)}) all-reduce(f32[]{:T(128)} %multiply_reduce_fusion, f32[]{:T(128)} %get-tuple-element.5, f32[]{:T(128)} %get-tuple-element.4), channel_id=1, replica_groups=mesh['gx'=4,'gy'=16,'gz'=8] {'gx','gy','gz'}, use_global_device_ids=true, to_apply=%region_5.7 | all-reduce | flops 3 | bytes 24 | tf_op jit(solution)/shard_map/psum | solution.py:124
  (253 shorter events, 63.8 us)
Async XLA Ops:
  0.6 7.9 %collective-permute-start.1 = (f32[1,1,1,3,128]{4,2,3,1,0:T(1,128)}, f32[1,1,1,3,128]{4,2,3,1,0:T(1,128)S(1)}, u32[]{:S(2)}, u32[]{:S(2)}) collective-permute-start(f32[1,1,1,3,128]{4,2,3,1,0:T(1,128)} %param.14), channel_id=1, source_target_pairs={{128,0},{256,128},{384,256},{129,1},{257,129},{385,257},{130,2},{2... | collective-permute-start | bytes 4616 | tf_op jit(solution)/shard_map/ppermute | solution.py:24
  2.1 5.8 collective-permute-start
  7.6 35.6 %copy-start.30 = (pred[256]{0:T(512)(128)(4,1)}, pred[256]{0:T(512)(128)(4,1)S(1)}, u32[]{:S(2)}) copy-start(pred[256]{0:T(512)(128)(4,1)S(1)} %get-tuple-element.93) | copy-start | bytes 772
  7.6 35.5 %copy-start.32 = (pred[256]{0:T(512)(128)(4,1)}, pred[256]{0:T(512)(128)(4,1)S(1)}, u32[]{:S(2)}) copy-start(pred[256]{0:T(512)(128)(4,1)S(1)} %get-tuple-element.94) | copy-start | bytes 772
  7.6 35.5 %copy-start.34 = (pred[256]{0:T(512)(128)(4,1)}, pred[256]{0:T(512)(128)(4,1)S(1)}, u32[]{:S(2)}) copy-start(pred[256]{0:T(512)(128)(4,1)S(1)} %get-tuple-element.99) | copy-start | bytes 772
  7.6 35.5 %copy-start.36 = (pred[256]{0:T(512)(128)(4,1)}, pred[256]{0:T(512)(128)(4,1)S(1)}, u32[]{:S(2)}) copy-start(pred[256]{0:T(512)(128)(4,1)S(1)} %get-tuple-element.100) | copy-start | bytes 772
  7.7 35.5 %copy-start.38 = (pred[256]{0:T(512)(128)(4,1)}, pred[256]{0:T(512)(128)(4,1)S(1)}, u32[]{:S(2)}) copy-start(pred[256]{0:T(512)(128)(4,1)S(1)} %get-tuple-element.95) | copy-start | bytes 772
  7.7 35.5 %copy-start.40 = (pred[256]{0:T(512)(128)(4,1)}, pred[256]{0:T(512)(128)(4,1)S(1)}, u32[]{:S(2)}) copy-start(pred[256]{0:T(512)(128)(4,1)S(1)} %get-tuple-element.96) | copy-start | bytes 772
  7.7 35.4 %copy-start.42 = (pred[256]{0:T(512)(128)(4,1)}, pred[256]{0:T(512)(128)(4,1)S(1)}, u32[]{:S(2)}) copy-start(pred[256]{0:T(512)(128)(4,1)S(1)} %get-tuple-element.97) | copy-start | bytes 772
  7.7 35.4 %copy-start.44 = (pred[256]{0:T(512)(128)(4,1)}, pred[256]{0:T(512)(128)(4,1)S(1)}, u32[]{:S(2)}) copy-start(pred[256]{0:T(512)(128)(4,1)S(1)} %get-tuple-element.98) | copy-start | bytes 772
  7.8 31.4 %copy-start.22 = (s32[1024]{0:T(1024)}, s32[1024]{0:T(1024)S(1)}, u32[]{:S(2)}) copy-start(s32[1024]{0:T(1024)S(1)} %get-tuple-element.91) | copy-start | bytes 12292
  7.8 33.3 %copy-start.21 = (s32[1024]{0:T(1024)}, s32[1024]{0:T(1024)S(1)}, u32[]{:S(2)}) copy-start(s32[1024]{0:T(1024)S(1)} %get-tuple-element.92) | copy-start | bytes 12292
  7.8 27.4 %copy-start.24 = (s32[1024]{0:T(1024)}, s32[1024]{0:T(1024)S(1)}, u32[]{:S(2)}) copy-start(s32[1024]{0:T(1024)S(1)} %get-tuple-element.89) | copy-start | bytes 12292
  7.8 29.4 %copy-start.23 = (s32[1024]{0:T(1024)}, s32[1024]{0:T(1024)S(1)}, u32[]{:S(2)}) copy-start(s32[1024]{0:T(1024)S(1)} %get-tuple-element.90) | copy-start | bytes 12292
  8.6 11.0 %collective-permute-start.3 = (f32[1,3,1,3,128]{4,2,3,1,0:T(1,128)S(1)}, f32[1,3,1,3,128]{4,2,3,1,0:T(1,128)S(1)}, u32[]{:S(2)}, u32[]{:S(2)}) collective-permute-start(f32[1,3,1,3,128]{4,2,3,1,0:T(1,128)S(1)} %constant_dynamic-update-slice_fusion), channel_id=1, source_target_pairs={{8,0},{16,8},{24,16},{32,24},{40,32},{48,40},{56,48},{64,56},{72,6... | collective-permute-start | bytes 13832 | tf_op jit(solution)/shard_map/ppermute | solution.py:24
  17.6 3.1 collective-permute-start.2
  20.7 5.3 collective-permute-start.5
  22.0 4.9 collective-permute-start.4
  47.7 27.8 %copy-start.12 = (bf16[3,8,32,256]{3,2,1,0:T(8,128)(2,1)S(1)}, bf16[3,8,32,256]{3,2,1,0:T(8,128)(2,1)}, u32[]{:S(2)}) copy-start(bf16[3,8,32,256]{3,2,1,0:T(8,128)(2,1)} %param.12) | copy-start | bytes 1179652
  47.7 5.3 collective-permute-start.6
  51.8 4.4 collective-permute-start.7
  56.3 8.7 %collective-permute-start.8 = (f32[8,34,1]{2,1,0:T(8,128)S(1)}, f32[8,34,1]{2,1,0:T(8,128)S(1)}, u32[]{:S(2)}, u32[]{:S(2)}) collective-permute-start(f32[8,34,1]{2,1,0:T(8,128)S(1)} %get-tuple-element.59), channel_id=1, source_target_pairs={{0,8},{8,16},{16,24},{24,32},{32,40},{40,48},{48,56},{56,64},{64,7... | collective-permute-start | bytes 3272 | tf_op jit(solution)/shard_map/ppermute | solution.py:22
  62.8 6.6 %collective-permute-start.9 = (f32[8,34,1]{2,1,0:T(8,128)S(1)}, f32[8,34,1]{2,1,0:T(8,128)S(1)}, u32[]{:S(2)}, u32[]{:S(2)}) collective-permute-start(f32[8,34,1]{2,1,0:T(8,128)S(1)} %get-tuple-element.60), channel_id=1, source_target_pairs={{8,0},{16,8},{24,16},{32,24},{40,32},{48,40},{56,48},{64,56},{72,6... | collective-permute-start | bytes 3272 | tf_op jit(solution)/shard_map/ppermute | solution.py:24
  69.6 5.9 collective-permute-start.10
  70.9 5.8 collective-permute-start.11
  78.5 3.0 collective-permute-start.12
  80.1 4.6 collective-permute-start.13
  85.0 9.8 %collective-permute-start.14 = (f32[3,8,34,1]{3,2,1,0:T(8,128)S(1)}, f32[3,8,34,1]{3,2,1,0:T(8,128)S(1)}, u32[]{:S(2)}, u32[]{:S(2)}) collective-permute-start(f32[3,8,34,1]{3,2,1,0:T(8,128)S(1)} %get-tuple-element.43), channel_id=1, source_target_pairs={{0,8},{8,16},{16,24},{24,32},{32,40},{40,48},{48,56},{56,64},{64,7... | collective-permute-start | bytes 9800 | tf_op jit(solution)/shard_map/ppermute | solution.py:22
  89.0 10.1 %collective-permute-start.15 = (f32[3,8,34,1]{3,2,1,0:T(8,128)S(1)}, f32[3,8,34,1]{3,2,1,0:T(8,128)S(1)}, u32[]{:S(2)}, u32[]{:S(2)}) collective-permute-start(f32[3,8,34,1]{3,2,1,0:T(8,128)S(1)} %get-tuple-element.44), channel_id=1, source_target_pairs={{8,0},{16,8},{24,16},{32,24},{40,32},{48,40},{56,48},{64,56},{72,6... | collective-permute-start | bytes 9800 | tf_op jit(solution)/shard_map/ppermute | solution.py:24
  99.4 7.5 %collective-permute-start.16 = (f32[3,1,34,258]{3,2,1,0:T(8,128)S(1)}, f32[3,1,34,258]{3,2,1,0:T(8,128)S(1)}, u32[]{:S(2)}, u32[]{:S(2)}) collective-permute-start(f32[3,1,34,258]{3,2,1,0:T(8,128)S(1)} %get-tuple-element.29), channel_id=1, source_target_pairs={{0,1},{1,2},{2,3},{3,4},{4,5},{5,6},{6,7},{8,9},{9,10},{10,11},{11... | collective-permute-start | bytes 315800 | tf_op jit(solution)/shard_map/ppermute | solution.py:22
  103.7 6.6 %collective-permute-start.17 = (f32[3,1,34,258]{3,2,1,0:T(8,128)S(1)}, f32[3,1,34,258]{3,2,1,0:T(8,128)S(1)}, u32[]{:S(2)}, u32[]{:S(2)}) collective-permute-start(f32[3,1,34,258]{3,2,1,0:T(8,128)S(1)} %get-tuple-element.30), channel_id=1, source_target_pairs={{1,0},{2,1},{3,2},{4,3},{5,4},{6,5},{7,6},{9,8},{10,9},{11,10},{12... | collective-permute-start | bytes 315800 | tf_op jit(solution)/shard_map/ppermute | solution.py:24
  113.2 198.5 %copy-start.29 = (f32[1,1,1,3,128]{4,2,3,1,0:T(1,128)S(1)}, f32[1,1,1,3,128]{4,2,3,1,0:T(1,128)}, u32[]{:S(2)}) copy-start(f32[1,1,1,3,128]{4,2,3,1,0:T(1,128)} %param.14) | copy-start | bytes 4612
  113.2 3.2 collective-permute-start.18
  115.1 4.5 collective-permute-start.19
  119.6 6.1 collective-permute-start.20
  123.8 5.6 collective-permute-start.21
  129.4 4.9 collective-permute-start.22
  132.9 6.8 %collective-permute-start.23 = (f32[1,5,5,3,128]{4,2,1,0,3:T(8,128)S(1)}, f32[1,5,5,3,128]{4,2,1,0,3:T(8,128)S(1)}, u32[]{:S(2)}, u32[]{:S(2)}) collective-permute-start(f32[1,5,5,3,128]{4,2,1,0,3:T(8,128)S(1)} %get-tuple-element.68), channel_id=1, source_target_pairs={{1,0},{2,1},{3,2},{4,3},{5,4},{6,5},{7,6},{9,8},{10,9},{11,10},{12... | collective-permute-start | bytes 115208 | tf_op jit(solution)/shard_map/ppermute | solution.py:24
  311.7 5.3 collective-permute-start.25
  313.0 4.7 collective-permute-start.24
  317.7 6.8 %collective-permute-start.27 = (f32[1,3,1,3,128]{4,2,3,1,0:T(1,128)S(1)}, f32[1,3,1,3,128]{4,2,3,1,0:T(1,128)S(1)}, u32[]{:S(2)}, u32[]{:S(2)}) collective-permute-start(f32[1,3,1,3,128]{4,2,3,1,0:T(1,128)S(1)} %pad_maximum_fusion.116), channel_id=1, source_target_pairs={{8,0},{16,8},{24,16},{32,24},{40,32},{48,40},{56,48},{64,56},{72,6... | collective-permute-start | bytes 13832 | tf_op jit(solution)/shard_map/ppermute | solution.py:24
  321.4 3.8 collective-permute-start.26
  325.2 5.3 collective-permute-start.29
  326.5 4.9 collective-permute-start.28
  354.3 28.3 %copy-start.1 = (f32[8,32,256]{2,1,0:T(8,128)}, f32[8,32,256]{2,1,0:T(8,128)S(1)}, u32[]{:S(2)}) copy-start(f32[8,32,256]{2,1,0:T(8,128)S(1)} %fusion.21) | copy-start | bytes 786436
  354.3 27.0 %copy-start.5 = (f32[8,32,256]{2,1,0:T(8,128)S(1)}, f32[8,32,256]{2,1,0:T(8,128)}, u32[]{:S(2)}) copy-start(f32[8,32,256]{2,1,0:T(8,128)} %get-tuple-element.23) | copy-start | bytes 786436
  354.4 6.0 collective-permute-start.31
  355.8 5.3 collective-permute-start.30
  361.3 8.4 %collective-permute-start.32 = (f32[8,34,1]{2,1,0:T(8,128)S(1)}, f32[8,34,1]{2,1,0:T(8,128)S(1)}, u32[]{:S(2)}, u32[]{:S(2)}) collective-permute-start(f32[8,34,1]{2,1,0:T(8,128)S(1)} %get-tuple-element.57), channel_id=1, source_target_pairs={{0,8},{8,16},{16,24},{24,32},{32,40},{40,48},{48,56},{56,64},{64,7... | collective-permute-start | bytes 3272 | tf_op jit(solution)/shard_map/ppermute | solution.py:22
  367.4 6.6 %collective-permute-start.33 = (f32[8,34,1]{2,1,0:T(8,128)S(1)}, f32[8,34,1]{2,1,0:T(8,128)S(1)}, u32[]{:S(2)}, u32[]{:S(2)}) collective-permute-start(f32[8,34,1]{2,1,0:T(8,128)S(1)} %get-tuple-element.58), channel_id=1, source_target_pairs={{8,0},{16,8},{24,16},{32,24},{40,32},{48,40},{56,48},{64,56},{72,6... | collective-permute-start | bytes 3272 | tf_op jit(solution)/shard_map/ppermute | solution.py:24
  374.2 5.9 collective-permute-start.34
  375.5 5.8 collective-permute-start.35
  382.9 5.2 collective-permute-start.36
  386.8 4.9 collective-permute-start.37
  391.9 9.7 %collective-permute-start.38 = (f32[3,8,34,1]{3,2,1,0:T(8,128)S(1)}, f32[3,8,34,1]{3,2,1,0:T(8,128)S(1)}, u32[]{:S(2)}, u32[]{:S(2)}) collective-permute-start(f32[3,8,34,1]{3,2,1,0:T(8,128)S(1)} %get-tuple-element.41), channel_id=1, source_target_pairs={{0,8},{8,16},{16,24},{24,32},{32,40},{40,48},{48,56},{56,64},{64,7... | collective-permute-start | bytes 9800 | tf_op jit(solution)/shard_map/ppermute | solution.py:22
  395.9 10.1 %collective-permute-start.39 = (f32[3,8,34,1]{3,2,1,0:T(8,128)S(1)}, f32[3,8,34,1]{3,2,1,0:T(8,128)S(1)}, u32[]{:S(2)}, u32[]{:S(2)}) collective-permute-start(f32[3,8,34,1]{3,2,1,0:T(8,128)S(1)} %get-tuple-element.42), channel_id=1, source_target_pairs={{8,0},{16,8},{24,16},{32,24},{40,32},{48,40},{56,48},{64,56},{72,6... | collective-permute-start | bytes 9800 | tf_op jit(solution)/shard_map/ppermute | solution.py:24
  406.3 6.9 %collective-permute-start.40 = (f32[3,1,34,258]{3,2,1,0:T(8,128)S(1)}, f32[3,1,34,258]{3,2,1,0:T(8,128)S(1)}, u32[]{:S(2)}, u32[]{:S(2)}) collective-permute-start(f32[3,1,34,258]{3,2,1,0:T(8,128)S(1)} %get-tuple-element.27), channel_id=1, source_target_pairs={{0,1},{1,2},{2,3},{3,4},{4,5},{5,6},{6,7},{8,9},{9,10},{10,11},{11... | collective-permute-start | bytes 315800 | tf_op jit(solution)/shard_map/ppermute | solution.py:22
  410.7 6.3 %collective-permute-start.41 = (f32[3,1,34,258]{3,2,1,0:T(8,128)S(1)}, f32[3,1,34,258]{3,2,1,0:T(8,128)S(1)}, u32[]{:S(2)}, u32[]{:S(2)}) collective-permute-start(f32[3,1,34,258]{3,2,1,0:T(8,128)S(1)} %get-tuple-element.28), channel_id=1, source_target_pairs={{1,0},{2,1},{3,2},{4,3},{5,4},{6,5},{7,6},{9,8},{10,9},{11,10},{12... | collective-permute-start | bytes 315800 | tf_op jit(solution)/shard_map/ppermute | solution.py:24
  420.6 4.9 collective-permute-start.42
  424.2 4.5 collective-permute-start.43
  428.8 6.5 %collective-permute-start.44 = (f32[3,5,1,3,128]{4,2,1,0,3:T(1,128)S(1)}, f32[3,5,1,3,128]{4,2,1,0,3:T(1,128)S(1)}, u32[]{:S(2)}, u32[]{:S(2)}) collective-permute-start(f32[3,5,1,3,128]{4,2,1,0,3:T(1,128)S(1)} %get-tuple-element.69), channel_id=1, source_target_pairs={{0,8},{8,16},{16,24},{24,32},{32,40},{40,48},{48,56},{56,64},{64,7... | collective-permute-start | bytes 69128 | tf_op jit(solution)/shard_map/ppermute | solution.py:22
  433.4 5.1 collective-permute-start.45
  438.5 4.6 collective-permute-start.46
  441.8 6.9 %collective-permute-start.47 = (f32[1,5,5,3,128]{4,2,1,0,3:T(8,128)S(1)}, f32[1,5,5,3,128]{4,2,1,0,3:T(8,128)S(1)}, u32[]{:S(2)}, u32[]{:S(2)}) collective-permute-start(f32[1,5,5,3,128]{4,2,1,0,3:T(8,128)S(1)} %get-tuple-element.66), channel_id=1, source_target_pairs={{1,0},{2,1},{3,2},{4,3},{5,4},{6,5},{7,6},{9,8},{10,9},{11,10},{12... | collective-permute-start | bytes 115208 | tf_op jit(solution)/shard_map/ppermute | solution.py:24
  (30 other events, 297.8 us)
where the time goes:
time: 623 us; the launch traced here: 621 us
  blocking collectives  337 us (54%)
  starting transfers between devices  141 us (23%)
  waiting for transfers between devices  76.9 us (12%)
  local copies, waits for them, and re-layouts  42 us (7%)
  other arithmetic  15.4 us (2%)
    psum x2, blocking collectives, on_device(): square_total = lax.psum(local_square, ('gx', 'gy', 'gz'))  337 us
    ppermute x24, starting transfers between devices, padded_2(): lax.ppermute(tail, axis, [(i, (i + 1) % count) for i in range(ends)])  95.2 us
    ppermute x24, waiting for transfers between devices, padded_2(): lax.ppermute(head, axis, [((i + 1) % count, i) for i in range(ends)])  58.9 us
    ppermute x24, starting transfers between devices, padded_2(): lax.ppermute(head, axis, [((i + 1) % count, i) for i in range(ends)])  45.6 us
    gather x16, local copies, waits for them, and re-layouts, on_device(): field = field + jnp.take(block_products, combined[:, slot_index], axis=0)  31.7 us
    ppermute x24, waiting for transfers between devices, padded_2(): lax.ppermute(tail, axis, [(i, (i + 1) % count) for i in range(ends)])  18 us
  transfers between devices with their start and end apart: 48, of which 29 were waited for; matrix products, arithmetic and copies ran while one was open for 0% of the time, Pallas kernels for 0%

commit v1 on v0

v1 whole, which is shorter than its diff:
```python
import functools

import jax
import jax.numpy as jnp
from jax import lax
from jax.experimental import pallas as pl
from jax.experimental.pallas import tpu as pltpu
from jax.sharding import PartitionSpec as P

MESH = pl.DeviceIdType.MESH
F32 = jnp.float32
BF16 = jnp.bfloat16
EDGE_SQUARED = 0.05
STEP_LENGTH = 0.05
NX, NY, NZ = 4, 16, 8
TZ, TX, TY, CP, NW = 8, 32, 256, 128, 8
ROWS = TZ * TX
REACH = 45
FIRST = 7
CENTRE = FIRST + 22
MAIN = FIRST + 9
HALO = 80


def split(x):
    high = x.astype(BF16)
    return high, (x - high.astype(F32)).astype(BF16)


def stacked(x):
    return jnp.concatenate(split(x), axis=0)


def dot(a, b):
    return jnp.dot(a, b, preferred_element_type=F32)


def dot_nt(a, b):
    return lax.dot_general(a, b, (((1,), (1,)), ((), ())), preferred_element_type=F32)


def iota(shape, dim):
    return lax.broadcasted_iota(jnp.int32, shape, dim)


def offset_of(i):
    group = i // 9
    rest = i - group * 9
    dy = (2 - group // 2) * (2 * (group % 2) - 1)
    dz = rest // 3 - 1
    dx = rest % 3 - 1
    return dz, dx, dy


def kernel(
    mi, mg, fg, vw, co, tb, cs, ws,
    out_c, out_w, out_e,
    NB, PB, RB, AP, AZ, CB, CBH, HZ, HX, XS, XC, YS, YR, P2, PT2, PY2, PYT2, MGS, YC, BHL,
    WP, WX, WY, IFS, FZ, PU, PUX, PYB, WG, GS, TF, TE, YT,
    nb_send, nb_recv, rb_send, rb_recv, face_send, face_recv, ap_send, ap_recv, az_send, az_recv,
):
    gx, gy, gz = lax.axis_index("gx"), lax.axis_index("gy"), lax.axis_index("gz")
    lane = iota((1, 128), 1)
    plane_at = gx * 8 + gy % 8
    ring_at = (gy // 8) * 8 + gz

    def plane_peer(r):
        other = (plane_at + r) % 32
        return (other // 8, (gy // 8) * 8 + other % 8, gz)

    def ring_peer(r):
        other = (ring_at + r) % 16
        return (gx, (other // 8) * 8 + gy % 8, other % 8)

    def neighbour(i):
        dz, dx, dy = offset_of(i)
        z, x, y = gz + dz, gx + dx, gy + dy
        there = (z >= 0) & (z < NZ) & (x >= 0) & (x < NX) & (y >= 0) & (y < NY) & (i != 40)
        u = (dy + 2) * 9 + (dz + 1) * 3 + dx + 1
        return there, (x, y, z), u

    def each(count, body, start=0):
        def step(i, carry):
            body(i)
            return carry

        lax.fori_loop(start, count, step, 0)

    for ref in (NB, RB, CB, CBH, HZ, HX, YR):
        ref[...] = jnp.zeros(ref.shape, ref.dtype)
    for c in range(3):
        NB[0, c, CENTRE : CENTRE + 1, :] = co[c : c + 1, :]

    barrier = pltpu.get_barrier_semaphore()

    def greet(i):
        there, where, _ = neighbour(i)

        @pl.when(there)
        def _():
            pl.semaphore_signal(barrier, inc=1, device_id=where, device_id_type=MESH)

    each(REACH, greet)

    def greet_plane(r):
        pl.semaphore_signal(barrier, inc=1, device_id=plane_peer(r), device_id_type=MESH)

    def greet_ring(r):
        pl.semaphore_signal(barrier, inc=1, device_id=ring_peer(r), device_id_type=MESH)

    each(16, greet_ring, 1)
    each(32, greet_plane, 1)

    slot = cs[...]
    third = (slot * 11) >> 5
    comb = ws[...] * 32 + (slot - 3 * third) * 9 + third
    CB[:, 0:8] = comb.astype(F32)
    four = [mi] + [mg.at[c] for c in range(3)]
    wide = [ref[...].astype(F32).reshape(ROWS, TY) for ref in four]
    for c in range(3):
        MGS[c, 0:ROWS, :] = wide[1 + c]
    for f, column in ((0, TY - 1), (1, 0)):
        packed = CB[...]
        for a in range(4):
            packed = jnp.where(lane == 8 + a, wide[a][:, column : column + 1], packed)
        YS[f] = packed.T[0:16, :]
    for f, row in ((0, TX - 1), (1, 0)):
        for z in range(TZ):
            m = z * TX + row
            for a in range(4):
                XS[f, a * 8 + z : a * 8 + z + 1, :] = wide[a][m : m + 1, :]
            XC[f, z : z + 1, :] = CB[m : m + 1, :]

    count_z = 3 - (gz == 0).astype(jnp.int32) - (gz == NZ - 1).astype(jnp.int32)
    count_x = 3 - (gx == 0).astype(jnp.int32) - (gx == NX - 1).astype(jnp.int32)
    count_y = jnp.minimum(gy, 2) + jnp.minimum(NY - 1 - gy, 2) + 1
    pl.semaphore_wait(barrier, count_z * count_x * count_y - 1 + 46)

    def block_copy(buffer_from, row_from, buffer_to, row_to, send, recv, where):
        return pltpu.make_async_remote_copy(
            src_ref=buffer_from.at[:, pl.ds(row_from, 1), :],
            dst_ref=buffer_to.at[:, pl.ds(row_to, 1), :],
            send_sem=send, recv_sem=recv, device_id=where, device_id_type=MESH,
        )

    def spread_copy(k, i):
        there, where, u = neighbour(i)
        return there, block_copy(
            NB.at[k], CENTRE, NB.at[k], FIRST + 44 - u, nb_send.at[k, u], nb_recv.at[k, 44 - u], where
        )

    def gather_copy(k, i):
        there, where, u = neighbour(i)
        return there, block_copy(
            PB.at[k], FIRST + u, RB.at[k], FIRST + 44 - u, rb_send.at[k, u], rb_recv.at[k, 44 - u], where
        )

    def start(maker, k):
        def body(i):
            there, copy = maker(k, i)
            pl.when(there)(copy.start)

        each(REACH, body)

    def finish_send(maker, k):
        def body(i):
            there, copy = maker(k, i)
            pl.when(there)(copy.wait_send)

        each(REACH, body)

    def finish_recv(buffer, recv, k):
        def body(i):
            there, where, u = neighbour(i)
            copy = block_copy(buffer.at[k], FIRST + u, buffer.at[k], FIRST + u, recv.at[k, u], recv.at[k, u], where)
            pl.when(there)(copy.wait_recv)

        each(REACH, body)

    def face_copies():
        result = []

        def add(n, src, dst, where, sends, gets):
            copy = pltpu.make_async_remote_copy(
                src_ref=src, dst_ref=dst, send_sem=face_send.at[n], recv_sem=face_recv.at[n],
                device_id=where, device_id_type=MESH,
            )
            result.append((copy, sends, gets))

        for f, side in ((0, 1), (1, -1)):
            ahead = (gy < NY - 1) if f == 0 else (gy > 0)
            behind = (gy > 0) if f == 0 else (gy < NY - 1)
            add(f, YS.at[f], YR.at[f], (gx, gy + side, gz), ahead, behind)
        for f, side in ((0, 1), (1, -1)):
            ahead = (gz < NZ - 1) if f == 0 else (gz > 0)
            behind = (gz > 0) if f == 0 else (gz < NZ - 1)
            at = TZ - 1 if f == 0 else 0
            where = (gx, gy, gz + side)
            add(2 + f, mi.at[at], HZ.at[f, 0], where, ahead, behind)
            add(4 + f, mg.at[:, at], HZ.at[f, pl.ds(1, 3)], where, ahead, behind)
            add(6 + f, CB.at[pl.ds(at * TX, TX)], CBH.at[pl.ds(f * TX, TX)], where, ahead, behind)
        for f, side in ((0, 1), (1, -1)):
            ahead = (gx < NX - 1) if f == 0 else (gx > 0)
            behind = (gx > 0) if f == 0 else (gx < NX - 1)
            where = (gx + side, gy, gz)
            add(8 + f, XS.at[f], HX.at[f], where, ahead, behind)
            add(10 + f, XC.at[f], CBH.at[pl.ds(64 + f * 8, 8)], where, ahead, behind)
        return result

    def sum_copy(buffer, k, at, where, send, recv):
        return pltpu.make_async_remote_copy(
            src_ref=buffer.at[k, pl.ds(at, 1)], dst_ref=buffer.at[k, pl.ds(at, 1)],
            send_sem=send.at[k], recv_sem=recv.at[k], device_id=where, device_id_type=MESH,
        )

    def sum_all(buffer, k, count, send, recv):
        return pltpu.make_async_remote_copy(
            src_ref=buffer.at[k, pl.ds(0, count)], dst_ref=buffer.at[k, pl.ds(0, count)],
            send_sem=send.at[k], recv_sem=recv.at[k], device_id=plane_peer(1), device_id_type=MESH,
        )

    faces = face_copies()
    for copy, sends, _ in faces[:2]:
        pl.when(sends)(copy.start)
    start(spread_copy, 0)
    for copy, sends, _ in faces[2:]:
        pl.when(sends)(copy.start)

    which = iota((256, 256), 0).astype(F32)

    def picked(rows):
        hit = jnp.zeros((256, rows.shape[1]), F32)
        for k in range(8):
            hit = hit + jnp.where(rows[k : k + 1, :] == which[:, 0 : rows.shape[1]], 1.0, 0.0)
        return hit

    own = picked(CB[...].T[0:8, :])
    PT2[:, 0:256] = own.astype(BF16)
    PT2[:, 384:640] = own.astype(BF16)
    own_t = own.T.astype(BF16)
    P2[0:256, 0:256] = own_t
    P2[0:256, 256:512] = own_t
    for c in range(3):
        for n in range(NW):
            TF[c * 16 + n : c * 16 + n + 1, :] = tb[n, TY - 16 : TY, :].astype(F32)[15:16, :]
            TF[c * 16 + 8 + n : c * 16 + 9 + n, :] = tb[n, 0:16, :].astype(F32)[0:1, :]
    TF[48:128, :] = jnp.zeros((80, CP), F32)
    TE[...] = TF[...].astype(BF16)
    fixed = [fg[c].astype(F32) for c in range(3)]
    IFS[...] = 1.0 / (fixed[0] * fixed[0] + fixed[1] * fixed[1] + fixed[2] * fixed[2] + EDGE_SQUARED)
    WG[...] = jnp.zeros(WG.shape, BF16)
    for at in (0, 1, 10, 11):
        FZ[at] = jnp.zeros((TX, TY), F32)
    PB[...] = jnp.zeros(PB.shape, F32)

    for copy, _, gets in faces:
        pl.when(gets)(copy.wait_recv)
    finish_recv(NB, nb_recv, 0)

    column = iota((1, 128), 1)
    shift = jnp.where(column < 32, -3.0, jnp.where(column < 64, 3.0, jnp.where(column < 72, -1.0, 1.0)))
    halo = picked(CBH[...].T[0:8, :] + shift)
    PT2[:, 256:384] = halo.astype(BF16)
    PT2[:, 640:768] = halo.astype(BF16)
    halo_t = halo.T.astype(BF16)
    P2[256:384, 0:256] = halo_t
    P2[256:384, 256:512] = halo_t
    for c in range(3):
        MGS[c, 256:288, :] = HZ[0, 1 + c].astype(F32)
        MGS[c, 288:320, :] = HZ[1, 1 + c].astype(F32)
        MGS[c, 320:328, :] = HX[0, 8 + c * 8 : 16 + c * 8, :]
        MGS[c, 328:336, :] = HX[1, 8 + c * 8 : 16 + c * 8, :]
    YT[...] = jnp.zeros((128, 256), F32)
    for f in range(2):
        for c in range(3):
            YT[c * 16 : c * 16 + 16, :] = jnp.broadcast_to(YR[f, 9 + c : 10 + c, :], (16, 256))
        YT[48:49, :] = YR[f, 8:9, :]
        YC[f] = YT[...].T
        side = picked(YR[f, 0:8, :])
        PYT2[f, :, 0:256] = side.astype(BF16)
        PYT2[f, :, 256:512] = side.astype(BF16)
        side_t = side.T.astype(BF16)
        PY2[f, :, 0:256] = side_t
        PY2[f, :, 256:512] = side_t

    def forward(k):
        near = stacked(jnp.concatenate([NB[k, c, MAIN : MAIN + 32, :] for c in range(3)], axis=0))
        for n in range(NW):
            product = dot_nt(near, tb[n])
            high, low = split(product[0:96] + product[96:192])
            for c in range(3):
                BHL[c, n * 32 : n * 32 + 32, :] = high[c * 32 : c * 32 + 32]
                BHL[c, 256 + n * 32 : 288 + n * 32, :] = low[c * 32 : c * 32 + 32]
        total = None
        for c in range(3):
            part = dot(P2[0:336, :], BHL[c]) * MGS[c]
            total = part if total is None else total + part
        wide_blocks = stacked(jnp.concatenate([NB[k, c] for c in range(3)], axis=0))
        ends = dot_nt(wide_blocks, TE[...])
        ends = ends[0:192] + ends[192:384]
        columns = []
        for f in range(2):
            at = FIRST + 18 * f
            chosen = jnp.zeros((32, 128), F32)
            for c in range(3):
                chosen = jnp.where(lane // 16 == c, ends[c * 64 + at : c * 64 + at + 32], chosen)
            spread = jnp.concatenate(
                [jnp.where(lane % 16 == n + 8 * f, chosen, 0.0) for n in range(NW)], axis=0
            )
            columns.append(jnp.sum(dot(PY2[f], stacked(spread)) * YC[f], axis=1, keepdims=True))
        return total, columns

    total, columns = forward(0)
    WP[1:9] = mi[...].astype(F32) + total[0:256].reshape(TZ, TX, TY)
    for f, at in ((0, 0), (1, 9)):
        WP[at] = HZ[f, 0].astype(F32) + total[256 + 32 * f : 288 + 32 * f]
        WX[f] = HX[f, 0:8, :] + total[320 + 8 * f : 328 + 8 * f]
        WY[f] = jnp.broadcast_to(YC[f, :, 48:49] + columns[f], (256, 128))

    row_at = iota((TX, TY), 0)
    lane_at = iota((TX, TY), 1)

    def backward(k):
        def plane(z, energy):
            here = WP[z + 1]
            rows = pl.ds(pl.multiple_of(z * TX, TX), TX)
            back_x, on_x = pltpu.roll(here, 1, 0), pltpu.roll(here, TX - 1, 0)
            back_x = jnp.where(row_at == 0, WX[0, pl.ds(z, 1), :], back_x)
            on_x = jnp.where(row_at == TX - 1, WX[1, pl.ds(z, 1), :], on_x)
            back_y, on_y = pltpu.roll(here, 1, 1), pltpu.roll(here, TY - 1, 1)
            side = WY[0, rows, :]
            back_y = jnp.where(lane_at == 0, jnp.concatenate([side, side], axis=1), back_y)
            side = WY[1, rows, :]
            on_y = jnp.where(lane_at == TY - 1, jnp.concatenate([side, side], axis=1), on_y)
            grads = (WP[z + 2] - WP[z], on_x - back_x, on_y - back_y)
            fixed = [fg[c, z].astype(F32) for c in range(3)]
            inner = (grads[0] * fixed[0] + grads[1] * fixed[1] + grads[2] * fixed[2]) * 0.5
            moving = (grads[0] * grads[0] + grads[1] * grads[1] + grads[2] * grads[2]) * 0.25 + EDGE_SQUARED
            inverse = 1.0 / moving
            weight = vw[z].astype(F32)
            scaled = weight * inner * IFS[z] * inverse
            term = weight - inner * scaled
            other = 0.5 * scaled * inner * inverse
            flux = [other * grads[c] - scaled * fixed[c] for c in range(3)]
            FZ[z + 2] = flux[0]
            pulled = jnp.where(row_at == 0, 0.0, pltpu.roll(flux[1], 1, 0))
            pulled = pulled - jnp.where(row_at == TX - 1, 0.0, pltpu.roll(flux[1], TX - 1, 0))
            pulled = pulled + jnp.where(lane_at == 0, 0.0, pltpu.roll(flux[2], 1, 1))
            pulled = pulled - jnp.where(lane_at == TY - 1, 0.0, pltpu.roll(flux[2], TY - 1, 1))
            PU[z] = pulled
            PUX[0, pl.ds(z, 1), :] = -flux[1][0:1, :]
            PUX[1, pl.ds(z, 1), :] = flux[1][TX - 1 : TX, :]
            PYB[0, rows, :] = jnp.broadcast_to(-flux[2][:, 0:1], (TX, 128))
            PYB[1, rows, :] = jnp.broadcast_to(flux[2][:, TY - 1 : TY], (TX, 128))
            return energy + term

        energy = lax.fori_loop(0, TZ, plane, jnp.zeros((TX, TY), F32))
        energy = jnp.sum(energy, axis=0, keepdims=True)

        def put(block, rows, at):
            for c in range(3):
                high, low = split(block * MGS[c, pl.ds(at, rows), :])
                WG[c, pl.ds(at, rows), :] = high
                WG[c, pl.ds(at + 384, rows), :] = low

        def weigh(z, carry):
            put(PU[z] + FZ[z + 1] - FZ[z + 3], TX, pl.multiple_of(z * TX, TX))
            return carry

        lax.fori_loop(0, TZ, weigh, 0)
        put(-FZ[2], TX, 256)
        put(FZ[9], TX, 288)
        put(jnp.concatenate([PUX[0], PUX[1]], axis=0), 16, 320)
        for c in range(3):
            high, low = split(dot(PT2[...], WG[c]))
            for n in range(NW):
                GS[c * 32 : c * 32 + 32, n * 256 : n * 256 + 256] = high[n * 32 : n * 32 + 32]
                GS[96 + c * 32 : 128 + c * 32, n * 256 : n * 256 + 256] = low[n * 32 : n * 32 + 32]
        partial = dot(GS[...], tb[...].reshape(NW * TY, CP))
        partial = partial[0:96] + partial[96:192]
        for c in range(3):
            PB[k, c, MAIN : MAIN + 32, :] = partial[c * 32 : c * 32 + 32]
        for f in range(2):
            drawn = jnp.where(lane < 48, PYB[f] * YC[f], 0.0)
            back = dot(PYT2[f], stacked(drawn))
            chosen = jnp.zeros((32, 128), F32)
            for n in range(NW):
                chosen = jnp.where(lane % 16 == n + 8 * f, back[n * 32 : n * 32 + 32], chosen)
            blocks = jnp.concatenate([jnp.where(lane // 16 == c, chosen, 0.0) for c in range(3)], axis=0)
            ends = dot(stacked(blocks), TE[...])
            ends = ends[0:96] + ends[96:192]
            at = FIRST + 18 * f
            for c in range(3):
                PB[k, c, at : at + 32, :] = PB[k, c, at : at + 32, :] + ends[c * 32 : c * 32 + 32]
        return energy[:, 0:128] + energy[:, 128:256]

    def reduce_gradient(k, energy):
        start(gather_copy, k)
        for c in range(3):
            RB[k, c, CENTRE : CENTRE + 1, :] = PB[k, c, CENTRE : CENTRE + 1, :]
        finish_recv(RB, rb_recv, k)
        gradient = [jnp.sum(RB[k, c], axis=0, keepdims=True) for c in range(3)]
        square = gradient[0] * gradient[0] + gradient[1] * gradient[1] + gradient[2] * gradient[2]
        energy = energy + pltpu.roll(energy, 64, 1)
        square = square + pltpu.roll(square, 64, 1)
        AP[k, pl.ds(plane_at, 1), :] = jnp.where(lane < 64, energy, square)
        each(32, lambda r: sum_copy(AP, k, plane_at, plane_peer(r), ap_send, ap_recv).start(), 1)
        return gradient

    def pass_on(k):
        sum_all(AP, k, 31, ap_send, ap_recv).wait_recv()
        AZ[k, pl.ds(ring_at, 1), :] = jnp.sum(AP[k], axis=0, keepdims=True)
        each(16, lambda r: sum_copy(AZ, k, ring_at, ring_peer(r), az_send, az_recv).start(), 1)

    def take_sum(k):
        sum_all(AZ, k, 15, az_send, az_recv).wait_recv()
        sums = jnp.sum(AZ[k], axis=0, keepdims=True)
        energy = jnp.sum(jnp.where(lane < 64, sums, 0.0), axis=1, keepdims=True)
        square = jnp.sum(jnp.where(lane < 64, 0.0, sums), axis=1, keepdims=True)
        devices = NX * NY * NZ
        step_size = STEP_LENGTH * lax.rsqrt(square * (1.0 / (devices * 3 * CP)) + 1e-06)
        return energy * (1.0 / (devices * TZ * TX * TY)), step_size

    energy = backward(0)
    first = reduce_gradient(0, energy)
    for c in range(3):
        NB[1, c, CENTRE : CENTRE + 1, :] = first[c]
    start(spread_copy, 1)
    pass_on(0)
    for copy, sends, _ in faces:
        pl.when(sends)(copy.wait_send)
    finish_send(spread_copy, 0)
    finish_recv(NB, nb_recv, 1)
    total, columns = forward(1)
    energy_0, size_0 = take_sum(0)
    WP[1:9] = WP[1:9] - size_0[0, 0] * total[0:256].reshape(TZ, TX, TY)
    for f, at in ((0, 0), (1, 9)):
        WP[at] = WP[at] - size_0 * total[256 + 32 * f : 288 + 32 * f]
        WX[f] = WX[f] - size_0 * total[320 + 8 * f : 328 + 8 * f]
        WY[f] = WY[f] - size_0 * columns[f]
    out_w[...] = WP[1:9]
    energy = backward(1)
    second = reduce_gradient(1, energy)
    finish_send(gather_copy, 0)
    finish_send(spread_copy, 1)
    sum_all(AP, 0, 31, ap_send, ap_recv).wait_send()
    sum_all(AZ, 0, 15, az_send, az_recv).wait_send()
    pass_on(1)
    finish_send(gather_copy, 1)
    sum_all(AP, 1, 31, ap_send, ap_recv).wait_send()
    energy_1, size_1 = take_sum(1)
    sum_all(AZ, 1, 15, az_send, az_recv).wait_send()
    for c in range(3):
        out_c[c : c + 1, :] = co[c : c + 1, :] - size_0 * first[c] - size_1 * second[c]
    out_e[0] = energy_0[0, 0]
    out_e[1] = energy_1[0, 0]


def on_device(moving_image, moving_grad, fixed_grad, voxel_weight, coefficients, weight_table, ctrl_slot, weight_slot):
    whole = pl.BlockSpec(memory_space=pltpu.VMEM)
    vmem = pltpu.VMEM
    sem = pltpu.SemaphoreType.DMA
    new, warped, energies = pl.pallas_call(
        kernel,
        out_shape=(
            jax.ShapeDtypeStruct((3, CP), F32),
            jax.ShapeDtypeStruct((TZ, TX, TY), F32),
            jax.ShapeDtypeStruct((2,), F32),
        ),
        in_specs=[whole] * 8,
        out_specs=(whole, whole, pl.BlockSpec(memory_space=pltpu.SMEM)),
        scratch_shapes=[
            vmem((2, 3, 64, CP), F32),
            vmem((2, 3, 64, CP), F32),
            vmem((2, 3, 64, CP), F32),
            vmem((2, 32, 128), F32),
            vmem((2, 16, 128), F32),
            vmem((256, 128), F32),
            vmem((128, 128), F32),
            vmem((2, 4, TX, TY), BF16),
            vmem((2, 32, TY), F32),
            vmem((2, 32, TY), F32),
            vmem((2, 8, 128), F32),
            vmem((2, 16, TY), F32),
            vmem((2, 16, TY), F32),
            vmem((384, 512), BF16),
            vmem((256, 768), BF16),
            vmem((2, 256, 512), BF16),
            vmem((2, 256, 512), BF16),
            vmem((3, 336, TY), F32),
            vmem((2, 256, 128), F32),
            vmem((3, 512, TY), BF16),
            vmem((10, TX, TY), F32),
            vmem((2, 8, TY), F32),
            vmem((2, 256, 128), F32),
            vmem((TZ, TX, TY), F32),
            vmem((12, TX, TY), F32),
            vmem((TZ, TX, TY), F32),
            vmem((2, 8, TY), F32),
            vmem((2, 256, 128), F32),
            vmem((3, 768, TY), BF16),
            vmem((192, 2048), BF16),
            vmem((128, CP), F32),
            vmem((128, CP), BF16),
            vmem((128, 256), F32),
            sem((2, REACH)), sem((2, REACH)), sem((2, REACH)), sem((2, REACH)),
            sem((12,)), sem((12,)), sem((2,)), sem((2,)), sem((2,)), sem((2,)),
        ],
        compiler_params=pltpu.CompilerParams(
            collective_id=0, has_side_effects=True, vmem_limit_bytes=48 * 1024 * 1024
        ),
    )(
        moving_image, moving_grad, fixed_grad, voxel_weight, coefficients.reshape(3, CP), weight_table,
        ctrl_slot.reshape(ROWS, 8), weight_slot.reshape(ROWS, 8),
    )
    return new.reshape(1, 1, 1, 3, CP), warped, energies


def solution(mesh):
    in_specs = (
        P("gz", "gx", "gy"),
        P(None, "gz", "gx", "gy"),
        P(None, "gz", "gx", "gy"),
        P("gz", "gx", "gy"),
        P("gz", "gx", "gy", None, None),
        P(),
        P("gz", "gx", "gy", None, None),
        P("gz", "gx", "gy", None, None),
    )
    out_specs = (P("gz", "gx", "gy", None, None), P("gz", "gx", "gy"), P())
    return jax.shard_map(on_device, mesh=mesh, in_specs=in_specs, out_specs=out_specs, check_vma=False)
```

time: 623 us -> 91.1 us (0.15)
  blocking collectives: 337 us -> 0 us
  starting transfers between devices: 141 us -> 0 us
  Pallas kernels: 0 us -> 83.2 us
  waiting for transfers between devices: 76.9 us -> 0 us
  local copies, waits for them, and re-layouts: 42 us -> 6.48 us
  other arithmetic: 15.4 us -> 0 us
    psum x2 -> x0, blocking collectives: 337 us -> none  [on_device(): square_total = lax.psum(local_square, ('gx', 'gy', 'gz'))]
    ppermute x48 -> x0, starting transfers between devices: 141 us -> none  [the longest x24 95.2 us: padded_2(): lax.ppermute(tail, axis, [(i, (i + 1) % count) for i in range(ends)])]
    pallas_call x0 -> x1, Pallas kernels: none -> 83.2 us  [on_device(): pl.pallas_call(kernel, out_shape=(jax.ShapeDtypeStruct((3, CP), F32), jax...]
    ppermute x48 -> x0, waiting for transfers between devices: 76.9 us -> none  [the longest x24 58.9 us: padded_2(): lax.ppermute(head, axis, [((i + 1) % count, i) for i in range(ends)])]
    gather x16 -> x0, local copies, waits for them, and re-layouts: 31.7 us -> none  [on_device(): field = field + jnp.take(block_products, combined[:, slot_index], axis=0)]
    add x6 -> x0, other arithmetic: 7.3 us -> none  [the longest x2 6.05 us: on_device(): field = field + jnp.take(block_products, combined[:, slot_index], axis=0)]
  transfers between devices with their start and end apart: 48 -> 0, of which waited for: 29 -> 0; matrix products, arithmetic and copies ran while one was open for 0% -> 0% of each run, Pallas kernels for 0% -> 0%
where the time goes in v1:
time: 91.1 us; the launch traced here: 90.4 us
  Pallas kernels  83.2 us (91%)
  local copies, waits for them, and re-layouts  6.48 us (7%)
    pallas_call x1, Pallas kernels, on_device(): pl.pallas_call(kernel, out_shape=(jax.ShapeDtypeStruct((3, CP), F32), jax...  83.2 us
    unnamed x18, local copies, waits for them, and re-layouts  6.48 us

profile of v1, /device:TPU:1, one launch (start us, length us, event | category | flops | bytes accessed | tf_op | source)
XLA Modules:
  0.0 90.4 jit_solution(9334666506421069119)
XLA Ops:
  0.6 0.7 copy.16
  1.3 0.0 copy-start.5
  1.3 0.0 copy-start.3
  1.3 0.0 copy-start.4
  1.3 0.9 copy.11
  2.2 0.0 copy-done.5
  2.2 0.1 copy.12
  2.3 0.0 copy-done.3
  2.3 0.0 copy-done.4
  2.3 0.0 copy-start
  2.4 1.0 %copy-done = bf16[8,256,128]{2,1,0:T(8,128)(2,1)S(1)} copy-done((bf16[8,256,128]{2,1,0:T(8,128)(2,1)S(1)}, bf16[8,256,128]{2,1,0:T(8,128)(2,1)}, u32[]{:S(2)}) %copy-start) | copy-done | bytes 524312
  3.4 0.0 copy-start.1
  3.4 1.0 %copy-done.1 = bf16[3,8,32,256]{3,2,1,0:T(8,128)(2,1)S(1)} copy-done((bf16[3,8,32,256]{3,2,1,0:T(8,128)(2,1)S(1)}, bf16[3,8,32,256]{3,2,1,0:T(8,128)(2,1)}, u32[]{:S(2)}) %copy-start.1) | copy-done | bytes 393240
  4.4 0.0 copy-start.2
  4.4 1.0 %copy-done.2 = bf16[3,8,32,256]{3,2,1,0:T(8,128)(2,1)S(1)} copy-done((bf16[3,8,32,256]{3,2,1,0:T(8,128)(2,1)S(1)}, bf16[3,8,32,256]{3,2,1,0:T(8,128)(2,1)}, u32[]{:S(2)}) %copy-start.2) | copy-done | bytes 393240
  5.4 83.2 %shard_map.103 = (f32[3,128]{1,0:T(4,128)S(1)}, f32[8,32,256]{2,1,0:T(8,128)S(1)}, f32[2]{0:T(128)S(1)}) custom-call(bf16[8,32,256]{2,1,0:T(8,128)(2,1)S(1)} %copy-done.3, bf16[3,8,32,256]{3,2,1,0:T(8,128)(2,1)S(1)} %copy-done.1, bf16[3,8,32,256]{3,2,1,0:T(8,128)(2,1)S(1)} %copy-done.2, bf16[8,32,256]{2,1,0:T(8,128)(2,1)S(1)} %copy-done.4, ...), custom_call_target="tpu_custom_call" | custom-call | tf_op jit(solution)/shard_map/pallas_call | solution.py:463
  88.6 0.6 copy.13
  89.2 0.7 copy.19
  89.9 0.5 copy.20
Async XLA Ops:
  1.3 0.9 copy-start.5
  1.3 1.0 %copy-start.3 = (bf16[8,32,256]{2,1,0:T(8,128)(2,1)S(1)}, bf16[8,32,256]{2,1,0:T(8,128)(2,1)}, u32[]{:S(2)}) copy-start(bf16[8,32,256]{2,1,0:T(8,128)(2,1)} %mi.1) | copy-start | bytes 393220
  1.3 1.0 %copy-start.4 = (bf16[8,32,256]{2,1,0:T(8,128)(2,1)S(1)}, bf16[8,32,256]{2,1,0:T(8,128)(2,1)}, u32[]{:S(2)}) copy-start(bf16[8,32,256]{2,1,0:T(8,128)(2,1)} %vw.1) | copy-start | bytes 393220
  2.3 1.0 %copy-start = (bf16[8,256,128]{2,1,0:T(8,128)(2,1)S(1)}, bf16[8,256,128]{2,1,0:T(8,128)(2,1)}, u32[]{:S(2)}) copy-start(bf16[8,256,128]{2,1,0:T(8,128)(2,1)} %tb.1) | copy-start | bytes 1572868
  3.4 1.0 %copy-start.1 = (bf16[3,8,32,256]{3,2,1,0:T(8,128)(2,1)S(1)}, bf16[3,8,32,256]{3,2,1,0:T(8,128)(2,1)}, u32[]{:S(2)}) copy-start(bf16[3,8,32,256]{3,2,1,0:T(8,128)(2,1)} %mg.1) | copy-start | bytes 1179652
  4.4 1.0 %copy-start.2 = (bf16[3,8,32,256]{3,2,1,0:T(8,128)(2,1)S(1)}, bf16[3,8,32,256]{3,2,1,0:T(8,128)(2,1)}, u32[]{:S(2)}) copy-start(bf16[3,8,32,256]{3,2,1,0:T(8,128)(2,1)} %fg.1) | copy-start | bytes 1179652

commit v2 on v1

--- a/solution.py
+++ b/solution.py
@@ -15,7 +15,6 @@
 NX, NY, NZ = 4, 16, 8
 TZ, TX, TY, CP, NW = 8, 32, 256, 128, 8
 ROWS = TZ * TX
-REACH = 45
 FIRST = 7
 CENTRE = FIRST + 22
 MAIN = FIRST + 9
@@ -43,27 +42,31 @@
     return lax.broadcasted_iota(jnp.int32, shape, dim)
 
 
-def offset_of(i):
-    group = i // 9
-    rest = i - group * 9
-    dy = (2 - group // 2) * (2 * (group % 2) - 1)
-    dz = rest // 3 - 1
-    dx = rest % 3 - 1
-    return dz, dx, dy
+NEAR = [
+    (dz, dx, dy) for dy in (2, -2, 1, -1, 0) for dx in (-1, 0, 1) for dz in (-1, 0, 1) if (dz, dx, dy) != (0, 0, 0)
+]
+COUNTS = sorted({a * b * c - 1 for a in (2, 3) for b in (2, 3) for c in (3, 4, 5)})
+
+
+def index_of(dz, dx, dy):
+    return (dy + 2) * 9 + (dz + 1) * 3 + dx + 1
 
 
 def kernel(
-    mi, mg, fg, vw, co, tb, cs, ws,
+    mi_in, mg_in, fg_in, vw_in, co_in, tb_in, cs_in, ws_in,
     out_c, out_w, out_e,
-    NB, PB, RB, AP, AZ, CB, CBH, HZ, HX, XS, XC, YS, YR, P2, PT2, PY2, PYT2, MGS, YC, BHL,
+    mi, mg, fg, vw, tb, cs, ws,
+    NB, PB, RB, AP, AZ, CT, HC, SEL, HZ, HX, XS, YS, YR, P2, PT2, PY2, PYT2, MGS, YC, BHL,
     WP, WX, WY, IFS, FZ, PU, PUX, PYB, WG, GS, TF, TE, YT,
-    nb_send, nb_recv, rb_send, rb_recv, face_send, face_recv, ap_send, ap_recv, az_send, az_recv,
+    in_sem, nb_send, nb_recv, rb_send, rb_recv, face_send, face_recv, ap_send, ap_recv, az_send, az_recv,
 ):
     gx, gy, gz = lax.axis_index("gx"), lax.axis_index("gy"), lax.axis_index("gz")
     lane = iota((1, 128), 1)
     plane_at = gx * 8 + gy % 8
     ring_at = (gy // 8) * 8 + gz
 
+    mine = (gx, gy, gz)
+
     def plane_peer(r):
         other = (plane_at + r) % 32
         return (other // 8, (gy // 8) * 8 + other % 8, gz)
@@ -72,69 +75,81 @@
         other = (ring_at + r) % 16
         return (gx, (other // 8) * 8 + gy % 8, other % 8)
 
-    def neighbour(i):
-        dz, dx, dy = offset_of(i)
-        z, x, y = gz + dz, gx + dx, gy + dy
-        there = (z >= 0) & (z < NZ) & (x >= 0) & (x < NX) & (y >= 0) & (y < NY) & (i != 40)
-        u = (dy + 2) * 9 + (dz + 1) * 3 + dx + 1
-        return there, (x, y, z), u
-
-    def each(count, body, start=0):
-        def step(i, carry):
-            body(i)
-            return carry
-
-        lax.fori_loop(start, count, step, 0)
-
-    for ref in (NB, RB, CB, CBH, HZ, HX, YR):
+    z_ok = {-1: gz > 0, 0: None, 1: gz < NZ - 1}
+    x_ok = {-1: gx > 0, 0: None, 1: gx < NX - 1}
+    y_ok = {-2: gy > 1, -1: gy > 0, 0: None, 1: gy < NY - 1, 2: gy < NY - 2}
+
+    def both(a, b):
+        return b if a is None else a if b is None else a & b
+
+    flat_ok = {(dz, dx): both(z_ok[dz], x_ok[dx]) for dz in z_ok for dx in x_ok}
+
+    def there(o):
+        return both(flat_ok[o[0], o[1]], y_ok[o[2]])
+
+    def id_of(o):
+        return (gx + o[1], gy + o[2], gz + o[0])
+
+    def fetch(n, src, dst):
+        copy = pltpu.make_async_copy(src, dst, in_sem.at[n])
+        copy.start()
+        return copy
+
+    for ref in (NB, RB, HC, HZ, HX, YR):
         ref[...] = jnp.zeros(ref.shape, ref.dtype)
-    for c in range(3):
-        NB[0, c, CENTRE : CENTRE + 1, :] = co[c : c + 1, :]
+    get_co = fetch(0, co_in, NB.at[0, :, pl.ds(CENTRE, 1), :])
+    get_cs = fetch(1, cs_in, cs)
+    get_ws = fetch(2, ws_in, ws)
+    get_mi = fetch(3, mi_in, mi)
+    get_mg = fetch(4, mg_in, mg)
+    get_tb = fetch(5, tb_in, tb)
+    get_fg = fetch(6, fg_in, fg)
+    get_vw = fetch(7, vw_in, vw)
 
     barrier = pltpu.get_barrier_semaphore()
 
-    def greet(i):
-        there, where, _ = neighbour(i)
-
-        @pl.when(there)
-        def _():
-            pl.semaphore_signal(barrier, inc=1, device_id=where, device_id_type=MESH)
-
-    each(REACH, greet)
-
-    def greet_plane(r):
-        pl.semaphore_signal(barrier, inc=1, device_id=plane_peer(r), device_id_type=MESH)
-
-    def greet_ring(r):
-        pl.semaphore_signal(barrier, inc=1, device_id=ring_peer(r), device_id_type=MESH)
-
-    each(16, greet_ring, 1)
-    each(32, greet_plane, 1)
-
+    def greet(where):
+        pl.semaphore_signal(barrier, inc=1, device_id=where, device_id_type=MESH)
+
+    for o in NEAR[:36]:
+        pl.when(there(o))(functools.partial(greet, id_of(o)))
+    for r in (8, 7, 9, 6, 10, 5, 11, 4, 12, 3, 13, 2, 14, 1, 15):
+        greet(ring_peer(r))
+    for r in range(1, 32):
+        greet(plane_peer(r))
+    for o in NEAR[36:]:
+        pl.when(there(o))(functools.partial(greet, id_of(o)))
+
+    get_cs.wait()
+    get_ws.wait()
     slot = cs[...]
     third = (slot * 11) >> 5
-    comb = ws[...] * 32 + (slot - 3 * third) * 9 + third
-    CB[:, 0:8] = comb.astype(F32)
-    four = [mi] + [mg.at[c] for c in range(3)]
-    wide = [ref[...].astype(F32).reshape(ROWS, TY) for ref in four]
-    for c in range(3):
-        MGS[c, 0:ROWS, :] = wide[1 + c]
-    for f, column in ((0, TY - 1), (1, 0)):
-        packed = CB[...]
-        for a in range(4):
-            packed = jnp.where(lane == 8 + a, wide[a][:, column : column + 1], packed)
-        YS[f] = packed.T[0:16, :]
-    for f, row in ((0, TX - 1), (1, 0)):
+    comb = (ws[...] * 32 + (slot - 3 * third) * 9 + third).astype(F32)
+    CT[...] = comb
+    YS[0, 0:8, :] = comb
+    YS[1, 0:8, :] = comb
+    YS[:, 8:16, :] = jnp.zeros((2, 8, TY), F32)
+    get_mi.wait()
+    get_mg.wait()
+    ends_at = iota((16, TY), 0)
+    ends = jnp.where(iota((16, TY), 1) == jnp.where(ends_at == 0, TY - 1, 0), jnp.where(ends_at < 2, 1.0, 0.0), 0.0)
+    ends = ends.astype(BF16)
+    for a in range(4):
+        rows = dot_nt(ends, (mi[...] if a == 0 else mg[a - 1]).reshape(ROWS, TY))
+        YS[0, 8 + a : 9 + a, :] = rows[0:1]
+        YS[1, 8 + a : 9 + a, :] = rows[1:2]
+    for a in range(4):
         for z in range(TZ):
-            m = z * TX + row
-            for a in range(4):
-                XS[f, a * 8 + z : a * 8 + z + 1, :] = wide[a][m : m + 1, :]
-            XC[f, z : z + 1, :] = CB[m : m + 1, :]
+            whole = mi[z] if a == 0 else mg[a - 1, z]
+            XS[0, a * 8 + z : a * 8 + z + 1, :] = whole.astype(F32)[TX - 1 : TX, :]
+            XS[1, a * 8 + z : a * 8 + z + 1, :] = whole.astype(F32)[0:1, :]
 
     count_z = 3 - (gz == 0).astype(jnp.int32) - (gz == NZ - 1).astype(jnp.int32)
     count_x = 3 - (gx == 0).astype(jnp.int32) - (gx == NX - 1).astype(jnp.int32)
     count_y = jnp.minimum(gy, 2) + jnp.minimum(NY - 1 - gy, 2) + 1
-    pl.semaphore_wait(barrier, count_z * count_x * count_y - 1 + 46)
+    near_count = count_z * count_x * count_y - 1
+    get_co.wait()
+    pl.semaphore_wait(barrier, near_count + 46)
 
     def block_copy(buffer_from, row_from, buffer_to, row_to, send, recv, where):
         return pltpu.make_async_remote_copy(
@@ -143,39 +158,26 @@
             send_sem=send, recv_sem=recv, device_id=where, device_id_type=MESH,
         )
 
-    def spread_copy(k, i):
-        there, where, u = neighbour(i)
-        return there, block_copy(
-            NB.at[k], CENTRE, NB.at[k], FIRST + 44 - u, nb_send.at[k, u], nb_recv.at[k, 44 - u], where
-        )
-
-    def gather_copy(k, i):
-        there, where, u = neighbour(i)
-        return there, block_copy(
-            PB.at[k], FIRST + u, RB.at[k], FIRST + 44 - u, rb_send.at[k, u], rb_recv.at[k, 44 - u], where
-        )
+    def spread_copy(k, o):
+        u = index_of(*o)
+        return block_copy(NB.at[k], CENTRE, NB.at[k], FIRST + 44 - u, nb_send.at[k], nb_recv.at[k], id_of(o))
+
+    def gather_copy(k, o):
+        u = index_of(*o)
+        return block_copy(PB.at[k], FIRST + u, RB.at[k], FIRST + 44 - u, rb_send.at[k], rb_recv.at[k], id_of(o))
 
     def start(maker, k):
-        def body(i):
-            there, copy = maker(k, i)
-            pl.when(there)(copy.start)
-
-        each(REACH, body)
-
-    def finish_send(maker, k):
-        def body(i):
-            there, copy = maker(k, i)
-            pl.when(there)(copy.wait_send)
-
-        each(REACH, body)
-
-    def finish_recv(buffer, recv, k):
-        def body(i):
-            there, where, u = neighbour(i)
-            copy = block_copy(buffer.at[k], FIRST + u, buffer.at[k], FIRST + u, recv.at[k, u], recv.at[k, u], where)
-            pl.when(there)(copy.wait_recv)
-
-        each(REACH, body)
+        for o in NEAR:
+            pl.when(there(o))(maker(k, o).start)
+
+    def all_blocks(buffer, k, send, recv, receive):
+        for count in COUNTS:
+            blocks = buffer.at[k, :, pl.ds(0, count), :]
+            copy = pltpu.make_async_remote_copy(
+                src_ref=blocks, dst_ref=blocks, send_sem=send.at[k], recv_sem=recv.at[k],
+                device_id=mine, device_id_type=MESH,
+            )
+            pl.when(near_count == count)(copy.wait_recv if receive else copy.wait_send)
 
     def face_copies():
         result = []
@@ -188,23 +190,17 @@
             result.append((copy, sends, gets))
 
         for f, side in ((0, 1), (1, -1)):
-            ahead = (gy < NY - 1) if f == 0 else (gy > 0)
-            behind = (gy > 0) if f == 0 else (gy < NY - 1)
-            add(f, YS.at[f], YR.at[f], (gx, gy + side, gz), ahead, behind)
+            add(f, YS.at[f], YR.at[f], id_of((0, 0, side)), y_ok[side], y_ok[-side])
         for f, side in ((0, 1), (1, -1)):
-            ahead = (gz < NZ - 1) if f == 0 else (gz > 0)
-            behind = (gz > 0) if f == 0 else (gz < NZ - 1)
             at = TZ - 1 if f == 0 else 0
-            where = (gx, gy, gz + side)
-            add(2 + f, mi.at[at], HZ.at[f, 0], where, ahead, behind)
-            add(4 + f, mg.at[:, at], HZ.at[f, pl.ds(1, 3)], where, ahead, behind)
-            add(6 + f, CB.at[pl.ds(at * TX, TX)], CBH.at[pl.ds(f * TX, TX)], where, ahead, behind)
+            where = id_of((side, 0, 0))
+            add(2 + f, mi.at[at], HZ.at[f, 0], where, z_ok[side], z_ok[-side])
+            add(4 + f, mg.at[:, at], HZ.at[f, pl.ds(1, 3)], where, z_ok[side], z_ok[-side])
+            add(6 + f, CT, HC.at[f], where, z_ok[side], z_ok[-side])
         for f, side in ((0, 1), (1, -1)):
-            ahead = (gx < NX - 1) if f == 0 else (gx > 0)
-            behind = (gx > 0) if f == 0 else (gx < NX - 1)
-            where = (gx + side, gy, gz)
-            add(8 + f, XS.at[f], HX.at[f], where, ahead, behind)
-            add(10 + f, XC.at[f], CBH.at[pl.ds(64 + f * 8, 8)], where, ahead, behind)
+            where = id_of((0, side, 0))
+            add(8 + f, XS.at[f], HX.at[f], where, x_ok[side], x_ok[-side])
+            add(10 + f, CT, HC.at[2 + f], where, x_ok[side], x_ok[-side])
         return result
 
     def sum_copy(buffer, k, at, where, send, recv):
@@ -234,18 +230,31 @@
             hit = hit + jnp.where(rows[k : k + 1, :] == which[:, 0 : rows.shape[1]], 1.0, 0.0)
         return hit
 
-    own = picked(CB[...].T[0:8, :])
+    for c in range(3):
+        MGS[c, 0:ROWS, :] = mg[c].astype(F32).reshape(ROWS, TY)
+    own = picked(CT[...])
     PT2[:, 0:256] = own.astype(BF16)
     PT2[:, 384:640] = own.astype(BF16)
     own_t = own.T.astype(BF16)
     P2[0:256, 0:256] = own_t
     P2[0:256, 256:512] = own_t
+    get_tb.wait()
     for c in range(3):
         for n in range(NW):
-            TF[c * 16 + n : c * 16 + n + 1, :] = tb[n, TY - 16 : TY, :].astype(F32)[15:16, :]
-            TF[c * 16 + 8 + n : c * 16 + 9 + n, :] = tb[n, 0:16, :].astype(F32)[0:1, :]
+            TF[c * 16 + n : c * 16 + n + 1, :] = tb[n].astype(F32)[TY - 1 : TY, :]
+            TF[c * 16 + 8 + n : c * 16 + 9 + n, :] = tb[n].astype(F32)[0:1, :]
     TF[48:128, :] = jnp.zeros((80, CP), F32)
     TE[...] = TF[...].astype(BF16)
+    at_m, at_lane = iota((256, 128), 0), iota((256, 128), 1)
+    for i, source in enumerate((
+        jnp.where(at_lane < 32, at_lane + 224, -1),
+        jnp.where((at_lane >= 32) & (at_lane < 64), at_lane - 32, -1),
+        jnp.where((at_lane >= 64) & (at_lane < 72), (at_lane - 64) * TX + TX - 1, -1),
+        jnp.where((at_lane >= 72) & (at_lane < 80), (at_lane - 72) * TX, -1),
+    )):
+        SEL[i] = jnp.where(at_m == source, 1.0, 0.0).astype(BF16)
+    get_fg.wait()
+    get_vw.wait()
     fixed = [fg[c].astype(F32) for c in range(3)]
     IFS[...] = 1.0 / (fixed[0] * fixed[0] + fixed[1] * fixed[1] + fixed[2] * fixed[2] + EDGE_SQUARED)
     WG[...] = jnp.zeros(WG.shape, BF16)
@@ -255,11 +264,15 @@
 
     for copy, _, gets in faces:
         pl.when(gets)(copy.wait_recv)
-    finish_recv(NB, nb_recv, 0)
+    all_blocks(NB, 0, nb_send, nb_recv, True)
 
     column = iota((1, 128), 1)
     shift = jnp.where(column < 32, -3.0, jnp.where(column < 64, 3.0, jnp.where(column < 72, -1.0, 1.0)))
-    halo = picked(CBH[...].T[0:8, :] + shift)
+    rows = None
+    for i in range(4):
+        part = dot(jnp.concatenate([HC[i], HC[i]], axis=0).astype(BF16), SEL[i])[0:8]
+        rows = part if rows is None else rows + part
+    halo = picked(rows + shift)
     PT2[:, 256:384] = halo.astype(BF16)
     PT2[:, 640:768] = halo.astype(BF16)
     halo_t = halo.T.astype(BF16)
@@ -398,19 +411,21 @@
         start(gather_copy, k)
         for c in range(3):
             RB[k, c, CENTRE : CENTRE + 1, :] = PB[k, c, CENTRE : CENTRE + 1, :]
-        finish_recv(RB, rb_recv, k)
+        all_blocks(RB, k, rb_send, rb_recv, True)
         gradient = [jnp.sum(RB[k, c], axis=0, keepdims=True) for c in range(3)]
         square = gradient[0] * gradient[0] + gradient[1] * gradient[1] + gradient[2] * gradient[2]
         energy = energy + pltpu.roll(energy, 64, 1)
         square = square + pltpu.roll(square, 64, 1)
         AP[k, pl.ds(plane_at, 1), :] = jnp.where(lane < 64, energy, square)
-        each(32, lambda r: sum_copy(AP, k, plane_at, plane_peer(r), ap_send, ap_recv).start(), 1)
+        for r in range(1, 32):
+            sum_copy(AP, k, plane_at, plane_peer(r), ap_send, ap_recv).start()
         return gradient
 
     def pass_on(k):
         sum_all(AP, k, 31, ap_send, ap_recv).wait_recv()
         AZ[k, pl.ds(ring_at, 1), :] = jnp.sum(AP[k], axis=0, keepdims=True)
-        each(16, lambda r: sum_copy(AZ, k, ring_at, ring_peer(r), az_send, az_recv).start(), 1)
+        for r in (8, 7, 9, 6, 10, 5, 11, 4, 12, 3, 13, 2, 14, 1, 15):
+            sum_copy(AZ, k, ring_at, ring_peer(r), az_send, az_recv).start()
 
     def take_sum(k):
         sum_all(AZ, k, 15, az_send, az_recv).wait_recv()
@@ -429,8 +444,8 @@
     pass_on(0)
     for copy, sends, _ in faces:
         pl.when(sends)(copy.wait_send)
-    finish_send(spread_copy, 0)
-    finish_recv(NB, nb_recv, 1)
+    all_blocks(NB, 0, nb_send, nb_recv, False)
+    all_blocks(NB, 1, nb_send, nb_recv, True)
     total, columns = forward(1)
     energy_0, size_0 = take_sum(0)
     WP[1:9] = WP[1:9] - size_0[0, 0] * total[0:256].reshape(TZ, TX, TY)
@@ -441,17 +456,17 @@
     out_w[...] = WP[1:9]
     energy = backward(1)
     second = reduce_gradient(1, energy)
-    finish_send(gather_copy, 0)
-    finish_send(spread_copy, 1)
+    all_blocks(RB, 0, rb_send, rb_recv, False)
+    all_blocks(NB, 1, nb_send, nb_recv, False)
     sum_all(AP, 0, 31, ap_send, ap_recv).wait_send()
     sum_all(AZ, 0, 15, az_send, az_recv).wait_send()
     pass_on(1)
-    finish_send(gather_copy, 1)
+    all_blocks(RB, 1, rb_send, rb_recv, False)
     sum_all(AP, 1, 31, ap_send, ap_recv).wait_send()
     energy_1, size_1 = take_sum(1)
     sum_all(AZ, 1, 15, az_send, az_recv).wait_send()
     for c in range(3):
-        out_c[c : c + 1, :] = co[c : c + 1, :] - size_0 * first[c] - size_1 * second[c]
+        out_c[c] = NB[0, c, CENTRE : CENTRE + 1, :] - size_0 * first[c] - size_1 * second[c]
     out_e[0] = energy_0[0, 0]
     out_e[1] = energy_1[0, 0]
 
@@ -463,24 +478,31 @@
     new, warped, energies = pl.pallas_call(
         kernel,
         out_shape=(
-            jax.ShapeDtypeStruct((3, CP), F32),
+            jax.ShapeDtypeStruct((3, 1, CP), F32),
             jax.ShapeDtypeStruct((TZ, TX, TY), F32),
             jax.ShapeDtypeStruct((2,), F32),
         ),
-        in_specs=[whole] * 8,
+        in_specs=[pl.BlockSpec(memory_space=pltpu.HBM)] * 8,
         out_specs=(whole, whole, pl.BlockSpec(memory_space=pltpu.SMEM)),
         scratch_shapes=[
+            vmem((TZ, TX, TY), BF16),
+            vmem((3, TZ, TX, TY), BF16),
+            vmem((3, TZ, TX, TY), BF16),
+            vmem((TZ, TX, TY), BF16),
+            vmem((NW, TY, CP), BF16),
+            vmem((8, ROWS), jnp.int32),
+            vmem((8, ROWS), jnp.int32),
             vmem((2, 3, 64, CP), F32),
             vmem((2, 3, 64, CP), F32),
             vmem((2, 3, 64, CP), F32),
             vmem((2, 32, 128), F32),
             vmem((2, 16, 128), F32),
-            vmem((256, 128), F32),
-            vmem((128, 128), F32),
+            vmem((8, ROWS), F32),
+            vmem((4, 8, ROWS), F32),
+            vmem((4, ROWS, 128), BF16),
             vmem((2, 4, TX, TY), BF16),
             vmem((2, 32, TY), F32),
             vmem((2, 32, TY), F32),
-            vmem((2, 8, 128), F32),
             vmem((2, 16, TY), F32),
             vmem((2, 16, TY), F32),
             vmem((384, 512), BF16),
@@ -503,15 +525,15 @@
             vmem((128, CP), F32),
             vmem((128, CP), BF16),
             vmem((128, 256), F32),
-            sem((2, REACH)), sem((2, REACH)), sem((2, REACH)), sem((2, REACH)),
+            sem((8,)), sem((2,)), sem((2,)), sem((2,)), sem((2,)),
             sem((12,)), sem((12,)), sem((2,)), sem((2,)), sem((2,)), sem((2,)),
         ],
         compiler_params=pltpu.CompilerParams(
-            collective_id=0, has_side_effects=True, vmem_limit_bytes=48 * 1024 * 1024
+            collective_id=0, has_side_effects=True, vmem_limit_bytes=63 * 1024 * 1024
         ),
     )(
-        moving_image, moving_grad, fixed_grad, voxel_weight, coefficients.reshape(3, CP), weight_table,
-        ctrl_slot.reshape(ROWS, 8), weight_slot.reshape(ROWS, 8),
+        moving_image, moving_grad, fixed_grad, voxel_weight, coefficients.reshape(3, 1, CP), weight_table,
+        ctrl_slot.reshape(ROWS, 8).T, weight_slot.reshape(ROWS, 8).T,
     )
     return new.reshape(1, 1, 1, 3, CP), warped, energies
 

time: 91.1 us -> 78.5 us (0.86)
  Pallas kernels: 83.2 us -> 74.3 us
  local copies, waits for them, and re-layouts: 6.48 us -> 3.42 us
    pallas_call x1, Pallas kernels: 83.2 us -> 74.3 us  [on_device(): pl.pallas_call(kernel, out_shape=(jax.ShapeDtypeStruct((3, 1, CP), F32),...]
    unnamed x18 -> x7, local copies, waits for them, and re-layouts: 6.48 us -> 3.42 us
where the time goes in v2:
time: 78.5 us; the launch traced here: 78.4 us
  Pallas kernels  74.3 us (95%)
  local copies, waits for them, and re-layouts  3.42 us (4%)
    pallas_call x1, Pallas kernels, on_device(): pl.pallas_call(kernel, out_shape=(jax.ShapeDtypeStruct((3, 1, CP), F32),...  74.3 us
    unnamed x7, local copies, waits for them, and re-layouts  3.42 us

profile of v2, /device:TPU:1, one launch (start us, length us, event | category | flops | bytes accessed | tf_op | source)
XLA Modules:
  0.0 78.4 jit_solution(14245445862729194655)
XLA Ops:
  0.6 74.3 %shard_map.103 = (f32[3,1,128]{2,1,0:T(1,128)}, f32[8,32,256]{2,1,0:T(8,128)}, f32[2]{0:T(128)}) custom-call(bf16[8,32,256]{2,1,0:T(8,128)(2,1)} %mi_in.1, bf16[3,8,32,256]{3,2,1,0:T(8,128)(2,1)} %mg_in.1, bf16[3,8,32,256]{3,2,1,0:T(8,128)(2,1)} %fg_in.1, bf16[8,32,256]{2,1,0:T(8,128)(2,1)} %vw_in.1, f32[3,1,128]{2,1,0:T(1,128)} %bitcast.12, ...), custom_call_target="tpu_custom_call" | custom-call | tf_op jit(solution)/shard_map/pallas_call | solution.py:478
  74.9 0.0 copy-start
  75.0 0.7 copy-done
  75.6 0.6 copy.15
  76.2 0.0 copy-start.1
  76.2 1.7 %copy.16 = f32[8,32,256]{2,1,0:T(8,128)} copy(f32[8,32,256]{2,1,0:T(8,128)} %get-tuple-element.16) | data formatting | bytes 524288
  77.9 0.0 copy-done.1
  77.9 0.5 copy.17
Async XLA Ops:
  74.9 0.7 copy-start
  76.2 1.7 %copy-start.1 = (f32[2]{0:T(128)S(1)}, f32[2]{0:T(128)}, u32[]{:S(2)}) copy-start(f32[2]{0:T(128)} %get-tuple-element.17) | copy-start | bytes 28

commit v3 on v2

--- a/solution.py
+++ b/solution.py
@@ -18,7 +18,7 @@
 FIRST = 7
 CENTRE = FIRST + 22
 MAIN = FIRST + 9
-HALO = 80
+UNROLL = 8
 
 
 def split(x):
@@ -43,13 +43,14 @@
 
 
 NEAR = [
-    (dz, dx, dy) for dy in (2, -2, 1, -1, 0) for dx in (-1, 0, 1) for dz in (-1, 0, 1) if (dz, dx, dy) != (0, 0, 0)
+    (dz, dx, dy) for dy in (2, 1, -2, -1, 0) for dx in (-1, 1, 0) for dz in (0, -1, 1) if (dz, dx, dy) != (0, 0, 0)
 ]
+REST = [o for o in NEAR if abs(o[2]) < 2]
+PLANE = sorted(
+    range(1, 32), key=lambda r: -(min(r // 8, 4 - r // 8) + min(r % 8 // 2, 4 - r % 8 // 2))
+)
+RING = (8, 7, 9, 6, 10, 5, 11, 4, 12, 3, 13, 2, 14, 1, 15)
 COUNTS = sorted({a * b * c - 1 for a in (2, 3) for b in (2, 3) for c in (3, 4, 5)})
-
-
-def index_of(dz, dx, dy):
-    return (dy + 2) * 9 + (dz + 1) * 3 + dx + 1
 
 
 def kernel(
@@ -77,7 +78,10 @@
 
     z_ok = {-1: gz > 0, 0: None, 1: gz < NZ - 1}
     x_ok = {-1: gx > 0, 0: None, 1: gx < NX - 1}
-    y_ok = {-2: gy > 1, -1: gy > 0, 0: None, 1: gy < NY - 1, 2: gy < NY - 2}
+    side_y = {-1: gy > 0, 1: gy < NY - 1}
+    toward = 1 - 2 * (gy // (NY // 2))
+    out = jnp.where(gy < NY // 2, gy, NY - 1 - gy)
+    y_ok = {-2: out > 1, -1: out > 0, 0: None, 1: None, 2: None}
 
     def both(a, b):
         return b if a is None else a if b is None else a & b
@@ -85,10 +89,14 @@
     flat_ok = {(dz, dx): both(z_ok[dz], x_ok[dx]) for dz in z_ok for dx in x_ok}
 
     def there(o):
-        return both(flat_ok[o[0], o[1]], y_ok[o[2]])
+        found = both(flat_ok[o[0], o[1]], y_ok[o[2]])
+        return gx >= 0 if found is None else found
 
     def id_of(o):
-        return (gx + o[1], gy + o[2], gz + o[0])
+        return (gx + o[1], gy + toward * o[2], gz + o[0])
+
+    def index_of(o):
+        return (toward * o[2] + 2) * 9 + ((o[0] + 1) * 3 + o[1] + 1)
 
     def fetch(n, src, dst):
         copy = pltpu.make_async_copy(src, dst, in_sem.at[n])
@@ -113,9 +121,9 @@
 
     for o in NEAR[:36]:
         pl.when(there(o))(functools.partial(greet, id_of(o)))
-    for r in (8, 7, 9, 6, 10, 5, 11, 4, 12, 3, 13, 2, 14, 1, 15):
+    for r in RING:
         greet(ring_peer(r))
-    for r in range(1, 32):
+    for r in PLANE:
         greet(plane_peer(r))
     for o in NEAR[36:]:
         pl.when(there(o))(functools.partial(greet, id_of(o)))
@@ -159,15 +167,15 @@
         )
 
     def spread_copy(k, o):
-        u = index_of(*o)
+        u = index_of(o)
         return block_copy(NB.at[k], CENTRE, NB.at[k], FIRST + 44 - u, nb_send.at[k], nb_recv.at[k], id_of(o))
 
     def gather_copy(k, o):
-        u = index_of(*o)
+        u = index_of(o)
         return block_copy(PB.at[k], FIRST + u, RB.at[k], FIRST + 44 - u, rb_send.at[k], rb_recv.at[k], id_of(o))
 
-    def start(maker, k):
-        for o in NEAR:
+    def start(maker, k, offsets=NEAR):
+        for o in offsets:
             pl.when(there(o))(maker(k, o).start)
 
     def all_blocks(buffer, k, send, recv, receive):
@@ -190,7 +198,7 @@
             result.append((copy, sends, gets))
 
         for f, side in ((0, 1), (1, -1)):
-            add(f, YS.at[f], YR.at[f], id_of((0, 0, side)), y_ok[side], y_ok[-side])
+            add(f, YS.at[f], YR.at[f], (gx, gy + side, gz), side_y[side], side_y[-side])
         for f, side in ((0, 1), (1, -1)):
             at = TZ - 1 if f == 0 else 0
             where = id_of((side, 0, 0))
@@ -262,9 +270,8 @@
         FZ[at] = jnp.zeros((TX, TY), F32)
     PB[...] = jnp.zeros(PB.shape, F32)
 
-    for copy, _, gets in faces:
+    for copy, _, gets in faces[2:]:
         pl.when(gets)(copy.wait_recv)
-    all_blocks(NB, 0, nb_send, nb_recv, True)
 
     column = iota((1, 128), 1)
     shift = jnp.where(column < 32, -3.0, jnp.where(column < 64, 3.0, jnp.where(column < 72, -1.0, 1.0)))
@@ -284,6 +291,8 @@
         MGS[c, 320:328, :] = HX[0, 8 + c * 8 : 16 + c * 8, :]
         MGS[c, 328:336, :] = HX[1, 8 + c * 8 : 16 + c * 8, :]
     YT[...] = jnp.zeros((128, 256), F32)
+    for copy, _, gets in faces[:2]:
+        pl.when(gets)(copy.wait_recv)
     for f in range(2):
         for c in range(3):
             YT[c * 16 : c * 16 + 16, :] = jnp.broadcast_to(YR[f, 9 + c : 10 + c, :], (16, 256))
@@ -295,6 +304,8 @@
         side_t = side.T.astype(BF16)
         PY2[f, :, 0:256] = side_t
         PY2[f, :, 256:512] = side_t
+
+    all_blocks(NB, 0, nb_send, nb_recv, True)
 
     def forward(k):
         near = stacked(jnp.concatenate([NB[k, c, MAIN : MAIN + 32, :] for c in range(3)], axis=0))
@@ -367,32 +378,8 @@
             PYB[1, rows, :] = jnp.broadcast_to(flux[2][:, TY - 1 : TY], (TX, 128))
             return energy + term
 
-        energy = lax.fori_loop(0, TZ, plane, jnp.zeros((TX, TY), F32))
+        energy = lax.fori_loop(0, TZ, plane, jnp.zeros((TX, TY), F32), unroll=UNROLL)
         energy = jnp.sum(energy, axis=0, keepdims=True)
-
-        def put(block, rows, at):
-            for c in range(3):
-                high, low = split(block * MGS[c, pl.ds(at, rows), :])
-                WG[c, pl.ds(at, rows), :] = high
-                WG[c, pl.ds(at + 384, rows), :] = low
-
-        def weigh(z, carry):
-            put(PU[z] + FZ[z + 1] - FZ[z + 3], TX, pl.multiple_of(z * TX, TX))
-            return carry
-
-        lax.fori_loop(0, TZ, weigh, 0)
-        put(-FZ[2], TX, 256)
-        put(FZ[9], TX, 288)
-        put(jnp.concatenate([PUX[0], PUX[1]], axis=0), 16, 320)
-        for c in range(3):
-            high, low = split(dot(PT2[...], WG[c]))
-            for n in range(NW):
-                GS[c * 32 : c * 32 + 32, n * 256 : n * 256 + 256] = high[n * 32 : n * 32 + 32]
-                GS[96 + c * 32 : 128 + c * 32, n * 256 : n * 256 + 256] = low[n * 32 : n * 32 + 32]
-        partial = dot(GS[...], tb[...].reshape(NW * TY, CP))
-        partial = partial[0:96] + partial[96:192]
-        for c in range(3):
-            PB[k, c, MAIN : MAIN + 32, :] = partial[c * 32 : c * 32 + 32]
         for f in range(2):
             drawn = jnp.where(lane < 48, PYB[f] * YC[f], 0.0)
             back = dot(PYT2[f], stacked(drawn))
@@ -405,10 +392,35 @@
             at = FIRST + 18 * f
             for c in range(3):
                 PB[k, c, at : at + 32, :] = PB[k, c, at : at + 32, :] + ends[c * 32 : c * 32 + 32]
+        start(gather_copy, k, [o for o in NEAR if abs(o[2]) == 2])
+
+        def put(block, rows, at):
+            for c in range(3):
+                high, low = split(block * MGS[c, pl.ds(at, rows), :])
+                WG[c, pl.ds(at, rows), :] = high
+                WG[c, pl.ds(at + 384, rows), :] = low
+
+        def weigh(z, carry):
+            put(PU[z] + FZ[z + 1] - FZ[z + 3], TX, pl.multiple_of(z * TX, TX))
+            return carry
+
+        lax.fori_loop(0, TZ, weigh, 0, unroll=UNROLL)
+        put(-FZ[2], TX, 256)
+        put(FZ[9], TX, 288)
+        put(jnp.concatenate([PUX[0], PUX[1]], axis=0), 16, 320)
+        for c in range(3):
+            high, low = split(dot(PT2[...], WG[c]))
+            for n in range(NW):
+                GS[c * 32 : c * 32 + 32, n * 256 : n * 256 + 256] = high[n * 32 : n * 32 + 32]
+                GS[96 + c * 32 : 128 + c * 32, n * 256 : n * 256 + 256] = low[n * 32 : n * 32 + 32]
+        partial = dot(GS[...], tb[...].reshape(NW * TY, CP))
+        partial = partial[0:96] + partial[96:192]
+        for c in range(3):
+            PB[k, c, MAIN : MAIN + 27, :] = PB[k, c, MAIN : MAIN + 27, :] + partial[c * 32 : c * 32 + 27]
         return energy[:, 0:128] + energy[:, 128:256]
 
     def reduce_gradient(k, energy):
-        start(gather_copy, k)
+        start(gather_copy, k, REST)
         for c in range(3):
             RB[k, c, CENTRE : CENTRE + 1, :] = PB[k, c, CENTRE : CENTRE + 1, :]
         all_blocks(RB, k, rb_send, rb_recv, True)
@@ -417,14 +429,14 @@
         energy = energy + pltpu.roll(energy, 64, 1)
         square = square + pltpu.roll(square, 64, 1)
         AP[k, pl.ds(plane_at, 1), :] = jnp.where(lane < 64, energy, square)
-        for r in range(1, 32):
+        for r in PLANE:
             sum_copy(AP, k, plane_at, plane_peer(r), ap_send, ap_recv).start()
         return gradient
 
     def pass_on(k):
         sum_all(AP, k, 31, ap_send, ap_recv).wait_recv()
         AZ[k, pl.ds(ring_at, 1), :] = jnp.sum(AP[k], axis=0, keepdims=True)
-        for r in (8, 7, 9, 6, 10, 5, 11, 4, 12, 3, 13, 2, 14, 1, 15):
+        for r in RING:
             sum_copy(AZ, k, ring_at, ring_peer(r), az_send, az_recv).start()
 
     def take_sum(k):

time: 78.5 us -> 73.6 us (0.938)
  Pallas kernels: 74.3 us -> 69.4 us
    pallas_call x1, Pallas kernels: 74.3 us -> 69.4 us  [on_device(): pl.pallas_call(kernel, out_shape=(jax.ShapeDtypeStruct((3, 1, CP), F32),...]
where the time goes in v3:
time: 73.6 us; the launch traced here: 73.5 us
  Pallas kernels  69.4 us (94%)
  local copies, waits for them, and re-layouts  3.42 us (5%)
    pallas_call x1, Pallas kernels, on_device(): pl.pallas_call(kernel, out_shape=(jax.ShapeDtypeStruct((3, 1, CP), F32),...  69.4 us
    unnamed x7, local copies, waits for them, and re-layouts  3.42 us

profile of v3, /device:TPU:1, one launch (start us, length us, event | category | flops | bytes accessed | tf_op | source)
XLA Modules:
  0.0 73.5 jit_solution(9679145356855732777)
XLA Ops:
  0.6 69.4 %shard_map.103 = (f32[3,1,128]{2,1,0:T(1,128)}, f32[8,32,256]{2,1,0:T(8,128)}, f32[2]{0:T(128)}) custom-call(bf16[8,32,256]{2,1,0:T(8,128)(2,1)} %mi_in.1, bf16[3,8,32,256]{3,2,1,0:T(8,128)(2,1)} %mg_in.1, bf16[3,8,32,256]{3,2,1,0:T(8,128)(2,1)} %fg_in.1, bf16[8,32,256]{2,1,0:T(8,128)(2,1)} %vw_in.1, f32[3,1,128]{2,1,0:T(1,128)} %bitcast.12, ...), custom_call_target="tpu_custom_call" | custom-call | tf_op jit(solution)/shard_map/pallas_call | solution.py:490
  70.1 0.0 copy-start
  70.1 0.7 copy-done
  70.7 0.6 copy.15
  71.3 0.0 copy-start.1
  71.3 1.7 %copy.16 = f32[8,32,256]{2,1,0:T(8,128)} copy(f32[8,32,256]{2,1,0:T(8,128)} %get-tuple-element.16) | data formatting | bytes 524288
  73.0 0.0 copy-done.1
  73.0 0.5 copy.17
Async XLA Ops:
  70.1 0.7 copy-start
  71.3 1.7 %copy-start.1 = (f32[2]{0:T(128)S(1)}, f32[2]{0:T(128)}, u32[]{:S(2)}) copy-start(f32[2]{0:T(128)} %get-tuple-element.17) | copy-start | bytes 28

commit v4 on v3

--- a/solution.py
+++ b/solution.py
@@ -481,6 +481,17 @@
         out_c[c] = NB[0, c, CENTRE : CENTRE + 1, :] - size_0 * first[c] - size_1 * second[c]
     out_e[0] = energy_0[0, 0]
     out_e[1] = energy_1[0, 0]
+
+
+def hand_over(new, warped, energies, out_c, out_w, out_e, done):
+    copies = [
+        pltpu.make_async_copy(src, dst, done.at[n])
+        for n, (src, dst) in enumerate(((warped, out_w), (new, out_c), (energies, out_e)))
+    ]
+    for copy in copies:
+        copy.start()
+    for copy in copies:
+        copy.wait()
 
 
 def on_device(moving_image, moving_grad, fixed_grad, voxel_weight, coefficients, weight_table, ctrl_slot, weight_slot):
@@ -547,6 +558,18 @@
         moving_image, moving_grad, fixed_grad, voxel_weight, coefficients.reshape(3, 1, CP), weight_table,
         ctrl_slot.reshape(ROWS, 8).T, weight_slot.reshape(ROWS, 8).T,
     )
+    hbm = pl.BlockSpec(memory_space=pltpu.HBM)
+    new, warped, energies = pl.pallas_call(
+        hand_over,
+        out_shape=(
+            jax.ShapeDtypeStruct((3, 1, CP), F32),
+            jax.ShapeDtypeStruct((TZ, TX, TY), F32),
+            jax.ShapeDtypeStruct((2,), F32),
+        ),
+        in_specs=[whole, whole, pl.BlockSpec(memory_space=pltpu.SMEM)],
+        out_specs=(hbm, hbm, hbm),
+        scratch_shapes=[sem((3,))],
+    )(new, warped, energies)
     return new.reshape(1, 1, 1, 3, CP), warped, energies
 
 

time: 73.6 us -> 71.9 us (0.977)
  local copies, waits for them, and re-layouts: 3.42 us -> 0 us
  Pallas kernels: 69.4 us -> 71.1 us
    unnamed x7 -> x0, local copies, waits for them, and re-layouts: 3.42 us -> none
    pallas_call x0 -> x1, Pallas kernels: none -> 1.7 us  [on_device(): pl.pallas_call(hand_over, out_shape=(jax.ShapeDtypeStruct((3, 1, CP), F32...]
where the time goes in v4:
time: 71.9 us; the launch traced here: 71.8 us
  Pallas kernels  71.1 us (99%)
    pallas_call x1, Pallas kernels, on_device(): pl.pallas_call(kernel, out_shape=(jax.ShapeDtypeStruct((3, 1, CP), F32),...  69.4 us
    pallas_call x1, Pallas kernels, on_device(): pl.pallas_call(hand_over, out_shape=(jax.ShapeDtypeStruct((3, 1, CP), F32...  1.7 us

profile of v4, /device:TPU:1, one launch (start us, length us, event | category | flops | bytes accessed | tf_op | source)
XLA Modules:
  0.0 71.8 jit_solution(17484352161573133419)
XLA Ops:
  0.6 69.4 %shard_map.103 = (f32[3,1,128]{2,1,0:T(1,128)}, f32[8,32,256]{2,1,0:T(8,128)}, f32[2]{0:T(128)}) custom-call(bf16[8,32,256]{2,1,0:T(8,128)(2,1)} %mi_in.1, bf16[3,8,32,256]{3,2,1,0:T(8,128)(2,1)} %mg_in.1, bf16[3,8,32,256]{3,2,1,0:T(8,128)(2,1)} %fg_in.1, bf16[8,32,256]{2,1,0:T(8,128)(2,1)} %vw_in.1, f32[3,1,128]{2,1,0:T(1,128)} %bitcast.12, ...), custom_call_target="tpu_custom_call" | custom-call | tf_op jit(solution)/shard_map/pallas_call | solution.py:501
  70.1 1.7 %shard_map.104 = (f32[3,1,128]{2,1,0:T(1,128)}, f32[8,32,256]{2,1,0:T(8,128)}, f32[2]{0:T(128)}) custom-call(f32[3,1,128]{2,1,0:T(1,128)} %get-tuple-element.9.new, f32[8,32,256]{2,1,0:T(8,128)} %get-tuple-element.10.warped, f32[2]{0:T(128)} %get-tuple-element.11.energies), custom_call_target="tpu_custom_call" | custom-call | tf_op jit(solution)/shard_map/pallas_call | solution.py:562

commit v5 on v4

--- a/solution.py
+++ b/solution.py
@@ -465,7 +465,8 @@
         WP[at] = WP[at] - size_0 * total[256 + 32 * f : 288 + 32 * f]
         WX[f] = WX[f] - size_0 * total[320 + 8 * f : 328 + 8 * f]
         WY[f] = WY[f] - size_0 * columns[f]
-    out_w[...] = WP[1:9]
+    put_w = pltpu.make_async_copy(WP.at[pl.ds(1, TZ)], out_w, in_sem.at[0])
+    put_w.start()
     energy = backward(1)
     second = reduce_gradient(1, energy)
     all_blocks(RB, 0, rb_send, rb_recv, False)
@@ -477,6 +478,7 @@
     sum_all(AP, 1, 31, ap_send, ap_recv).wait_send()
     energy_1, size_1 = take_sum(1)
     sum_all(AZ, 1, 15, az_send, az_recv).wait_send()
+    put_w.wait()
     for c in range(3):
         out_c[c] = NB[0, c, CENTRE : CENTRE + 1, :] - size_0 * first[c] - size_1 * second[c]
     out_e[0] = energy_0[0, 0]
@@ -506,7 +508,7 @@
             jax.ShapeDtypeStruct((2,), F32),
         ),
         in_specs=[pl.BlockSpec(memory_space=pltpu.HBM)] * 8,
-        out_specs=(whole, whole, pl.BlockSpec(memory_space=pltpu.SMEM)),
+        out_specs=(whole, pl.BlockSpec(memory_space=pltpu.HBM), pl.BlockSpec(memory_space=pltpu.SMEM)),
         scratch_shapes=[
             vmem((TZ, TX, TY), BF16),
             vmem((3, TZ, TX, TY), BF16),

time: 71.9 us -> 71.8 us (level)
  no operation moved by 1% of the time
where the time goes in v5:
time: 71.8 us; the launch traced here: 71.7 us
  Pallas kernels  71 us (99%)
    pallas_call x1, Pallas kernels, on_device(): pl.pallas_call(kernel, out_shape=(jax.ShapeDtypeStruct((3, 1, CP), F32),...  69.3 us
    pallas_call x1, Pallas kernels, on_device(): pl.pallas_call(hand_over, out_shape=(jax.ShapeDtypeStruct((3, 1, CP), F32...  1.7 us

profile of v5, /device:TPU:1, one launch (start us, length us, event | category | flops | bytes accessed | tf_op | source)
XLA Modules:
  0.0 71.7 jit_solution(17669646338428932385)
XLA Ops:
  0.6 69.3 %shard_map.103 = (f32[3,1,128]{2,1,0:T(1,128)}, f32[8,32,256]{2,1,0:T(8,128)}, f32[2]{0:T(128)}) custom-call(bf16[8,32,256]{2,1,0:T(8,128)(2,1)} %mi_in.1, bf16[3,8,32,256]{3,2,1,0:T(8,128)(2,1)} %mg_in.1, bf16[3,8,32,256]{3,2,1,0:T(8,128)(2,1)} %fg_in.1, bf16[8,32,256]{2,1,0:T(8,128)(2,1)} %vw_in.1, f32[3,1,128]{2,1,0:T(1,128)} %bitcast.12, ...), custom_call_target="tpu_custom_call" | custom-call | tf_op jit(solution)/shard_map/pallas_call | solution.py:503
  70.0 1.7 %shard_map.104 = (f32[3,1,128]{2,1,0:T(1,128)}, f32[8,32,256]{2,1,0:T(8,128)}, f32[2]{0:T(128)}) custom-call(f32[3,1,128]{2,1,0:T(1,128)} %get-tuple-element.9.new, f32[8,32,256]{2,1,0:T(8,128)} %get-tuple-element.10.warped, f32[2]{0:T(128)} %get-tuple-element.11.energies), custom_call_target="tpu_custom_call" | custom-call | tf_op jit(solution)/shard_map/pallas_call | solution.py:564
